TPU v7x, 128 devices: a whole 4x4x4 slice. The times are simulated.
128 devices in a mesh: vv: 64 (over z, y, x_hi, core), grp: 2 (over x_lo).
Axes of the slice: x: 4 (x_hi: 2, x_lo: 2; x = x_hi * 2 + x_lo), y: 4, z: 4, core: 2. Of those that a mesh axis runs over, the one named last changes fastest.
Arguments:
- integrals: bfloat16 [64, 4608, 1536], P('vv', 'grp'), may hold values from -0.15625 to 0.15625
- amplitudes: bfloat16 [2048, 12288], P('grp'), may hold values from -6 to 6
- orbital_irrep: int32 [768], replicated, may hold values from 0 to 7, as said below
- pair_irrep: int32 [64], P('vv'), may hold values from 0 to 7, as said below
- panel_block: int32 [1], replicated, may hold values from 0 to 7
Outputs:
- residual: bfloat16 [2048, 64, 4608], P('vv', None, 'grp')
Inputs may be any that keep to these rules, and one draw needn't show every extreme that they name: `orbital_irrep`: constant over each aligned run of 96 orbitals; the 8 runs carry different irreps. `pair_irrep`: every irrep is owned by some index.
All inputs are finite; a program needn't handle non-finite values.
Results may differ from a plain program's by a relative error of at most 0.001.
Values may be sent and summed in bfloat16 or wider, within the bound.
A program may use at most 256 MiB of HBM per device.

v0:
```python
import jax
import jax.numpy as jnp
from jax import lax
from jax.sharding import PartitionSpec as P

NIRR = 8
BS = 96
DW = 16


def shards(integrals, amplitudes, orbital_irrep, pair_irrep, panel_block):
    block_irrep = orbital_irrep.reshape(NIRR, BS)[:, 0]
    block_index = jnp.arange(NIRR, dtype=jnp.int32)
    panel_irrep = jnp.sum(jnp.where(block_index == panel_block[0], block_irrep, 0))
    target = jnp.bitwise_xor(pair_irrep[0], panel_irrep)
    allowed = jnp.sum(jnp.where(block_irrep == target, block_index, 0))
    integral_rows = integrals[0]
    rows_here = amplitudes.shape[0]
    shaped = amplitudes.reshape(rows_here, DW, NIRR, BS)
    partial_value = jnp.einsum(
        "ik,rk->ir",
        lax.all_gather(
            lax.dynamic_slice_in_dim(shaped, allowed, 1, 2).reshape(rows_here, DW * BS),
            "grp",
            axis=0,
            tiled=True,
        ),
        integral_rows,
        preferred_element_type=jnp.float32,
    )
    local_part = partial_value.astype(jnp.bfloat16)[:, None, :]
    return lax.all_to_all(local_part, "vv", split_axis=0, concat_axis=1, tiled=True)


def solution(mesh):
    return jax.shard_map(
        shards,
        mesh=mesh,
        in_specs=(P("vv", "grp", None), P("grp", None), P(), P("vv"), P()),
        out_specs=P("vv", None, "grp"),
        check_vma=False,
    )
```

profile of v0, /device:TPU:1, one launch (start us, length us, event | category | flops | bytes accessed | tf_op | source)
XLA Modules:
  0.0 375.1 jit_solution(12353991858488157393)
XLA Ops:
  6.5 0.0 all-gather.2.cloned.1.call-start
  6.5 0.8 reshape.10
  7.3 0.1 slice_reduce_fusion
  8.7 0.6 fusion.2
  9.9 0.6 fusion.3
  11.8 32.6 %copy.14 = bf16[1024,12288]{0,1:T(8,128)(2,1)} copy(bf16[1024,12288]{1,0:T(8,128)(2,1)} %param.6) | data formatting | bytes 50331648 | tf_op args[1]
  45.1 4.0 %constant_dynamic-slice_fusion = bf16[1024,16,1,96]{0,3,2,1:T(8,128)(2,1)} fusion(bf16[1024,16,8,96]{0,3,2,1:T(8,128)(2,1)} %bitcast.18, s32[]{:T(128)S(6)} %select_n.12), kind=kLoop, calls=%fused_computation.8 | loop fusion | bytes 6291460 | tf_op jit(solution)/shard_map/dynamic_slice | solution.py:23
  49.1 0.0 all-gather.2.cloned.1.call-update
  49.1 86.3 %all-gather.2.cloned.1.call-done = bf16[2048,1536]{0,1:T(8,128)(2,1)} async-done(((bf16[1024,1536]{0,1:T(8,128)(2,1)}), bf16[2048,1536]{0,1:T(8,128)(2,1)}) %all-gather.2.cloned.1.call-update) | async-done | bytes 6291472 | tf_op jit(solution)/shard_map/all_gather | solution.py:22
  135.4 21.2 %fusion = bf16[2048,1,2304]{2,0,1:T(8,128)(2,1)} fusion(bf16[2048,1536]{0,1:T(8,128)(2,1)} %all-gather.2.cloned.1.call-done, bf16[1,2304,1536]{2,1,0:T(8,128)(2,1)} %param.5), kind=kOutput, calls=%fused_computation.1 | convolution fusion | flops 14500233216 | bytes 22806528 | tf_op jit(solution)/shard_map/ik,rk->ir/dot_general | solution.py:20
  156.6 0.6 broadcast.1
  157.2 12.1 %reduce.2 = bf16[2048,2304]{1,0:T(8,128)(2,1)} reduce(bf16[2048,1,2304]{2,0,1:T(8,128)(2,1)} %fusion, bf16[]{:T(256)} %broadcast.1), dimensions={1}, to_apply=%copy.15.reduce_sub_computation | reduce | bytes 18874370 | tf_op jit(solution)/shard_map/broadcast_in_dim | solution.py:31
  169.2 13.0 %reshape.13 = bf16[64,2,36864]{2,1,0:T(2,128)(2,1)} reshape(bf16[2048,2304]{1,0:T(8,128)(2,1)} %reduce.2) | data formatting | bytes 18874368
  182.2 120.0 %all_to_all.18 = bf16[64,2,36864]{2,1,0:T(2,128)(2,1)} all-to-all(bf16[64,2,36864]{2,1,0:T(2,128)(2,1)} %reshape.13), channel_id=1, replica_groups=mesh['vv'=64,'grp'=2] {'vv'}, dimensions={0} | all-to-all | bytes 18874368 | tf_op jit(solution)/shard_map/all_to_all | solution.py:32
  302.3 39.1 %reshape.14 = bf16[2048,1,2304]{2,1,0:T(2,128)(2,1)} reshape(bf16[64,2,36864]{2,1,0:T(2,128)(2,1)} %all_to_all.18) | data formatting | bytes 18874368
  341.4 14.2 %copy.17 = bf16[2048,1,2304]{2,0,1:T(8,128)(2,1)} copy(bf16[2048,1,2304]{2,1,0:T(2,128)(2,1)} %reshape.14) | data formatting | bytes 18874368
  355.6 12.7 %copy.16 = bf16[32,64,2304]{2,1,0:T(8,128)(2,1)} copy(bf16[32,64,2304]{2,0,1:T(8,128)(2,1)} %bitcast.17) | data formatting | bytes 18874368 | tf_op jit(solution)/shard_map/all_to_all | solution.py:32
Async XLA Ops:
  6.5 128.9 %all-gather.2.cloned.1.call-start = ((), (), s32[]{:S(2)}) async-start(), calls=%async_computation.1 | async-start | bytes 9437184 | tf_op jit(solution)/shard_map/all_gather | solution.py:22
Sparse Core Ops, SparseCore 0:
  49.3 86.0 all-gather.1
where the time goes:
time: 378 us; the launch traced here: 375 us
  blocking collectives  120 us (32%)
  local copies, waits for them, and re-layouts  117 us (31%)
  waiting for transfers between devices  86.3 us (23%)
  matrix products  21.2 us (6%)
  between operations  17.2 us (5%)
  other arithmetic  13.3 us (4%)
    all_to_all x1, blocking collectives, shards(): lax.all_to_all(local_part, 'vv', split_axis=0, concat_axis=1, tiled=True)  120 us
    unnamed x4, local copies, waits for them, and re-layouts  99 us
    all_gather x1, waiting for transfers between devices, shards(): lax.all_gather(lax.dynamic_slice_in_dim(shaped, allowed, 1, 2).reshape(ro...  86.3 us
    dot_general x1, matrix products, shards(): jnp.einsum('ik,rk->ir', lax.all_gather(lax.dynamic_slice_in_dim(shaped, a...  21.2 us
    all_to_all x1, local copies, waits for them, and re-layouts, shards(): lax.all_to_all(local_part, 'vv', split_axis=0, concat_axis=1, tiled=True)  12.7 us
    broadcast_in_dim x1, other arithmetic, shards(): local_part = partial_value.astype(jnp.bfloat16)[:, None, :]  12.1 us
  transfers between devices with their start and end apart: 1, of which 1 were waited for; matrix products, arithmetic and copies ran while one was open for 0% of the time, Pallas kernels for 0%

commit v1 on v0

v1 whole, which is shorter than its diff:
```python
import functools

import jax
import jax.numpy as jnp
from jax import lax
from jax.experimental import pallas as pl
from jax.experimental.pallas import tpu as pltpu
from jax.sharding import PartitionSpec as P

NIRR = 8
BS = 96
DW = 16
NV = NIRR * BS
KP = DW * BS
ROWS = 2304
IJ = 2048
HALF = IJ // 2
N_VV = 64
OWN = IJ // N_VV
BLOCK = 256
PER_BLOCK = BLOCK // OWN
CHUNK = 128
NCOL = 768
MESH = pl.DeviceIdType.MESH
SLICE_ROWS = 256
MIB = 1024 * 1024


def slice_kernel(row0, nblocks, orb, pair, panel, amp, out, win, outbuf, in_sem, out_sem):
    target = pair[0] ^ orb[panel[0] * BS]
    allowed = jnp.int32(0)
    for k in range(NIRR):
        allowed += jnp.where(orb[k * BS] == target, jnp.int32(k), jnp.int32(0))
    tile = jnp.minimum(allowed * BS // 128, 4)
    off = allowed * BS - tile * 128

    def window(b, d):
        return pltpu.make_async_copy(
            amp.at[pl.ds(row0 + b * SLICE_ROWS, SLICE_ROWS), pl.ds(pl.multiple_of(d * NV + tile * 128, 128), 256)],
            win.at[b, d],
            in_sem.at[b],
        )

    def result(b):
        return pltpu.make_async_copy(outbuf.at[b], out.at[pl.ds(b * SLICE_ROWS, SLICE_ROWS)], out_sem.at[b])

    for b in range(nblocks):
        for d in range(DW):
            window(b, d).start()
    lane = lax.broadcasted_iota(jnp.int32, (SLICE_ROWS, 128), 1)

    for b in range(nblocks):
        for d in range(DW):
            window(b, d).wait()

        @pl.loop(0, DW // 4)
        def _(q):
            w = [
                pltpu.roll(win[b, q * 4 + j].astype(jnp.float32), lax.rem((96 * j) % 128 - off + 512, 256), 1)
                for j in range(4)
            ]
            t0 = jnp.where(lane < 96, w[0][:, :128], w[1][:, :128])
            t1 = jnp.where(lane < 64, w[1][:, 128:], w[2][:, :128])
            t2 = jnp.where(lane < 32, w[2][:, 128:], w[3][:, :128])
            base = pl.multiple_of(q * 384, 128)
            outbuf[b, :, pl.ds(base, 384)] = jnp.concatenate([t0, t1, t2], axis=1).astype(jnp.bfloat16)

        result(b).start()
    for b in range(nblocks):
        result(b).wait()


def slice_block(row0, rows, orb, pair, panel, amp):
    nblocks = rows // SLICE_ROWS
    smem = pl.BlockSpec(memory_space=pltpu.SMEM)
    hbm = pl.BlockSpec(memory_space=pl.ANY)
    return pl.pallas_call(
        functools.partial(slice_kernel, row0, nblocks),
        name="slice_block",
        out_shape=jax.ShapeDtypeStruct((rows, KP), jnp.bfloat16),
        in_specs=[smem, smem, smem, hbm],
        out_specs=hbm,
        scratch_shapes=[
            pltpu.VMEM((nblocks, DW, SLICE_ROWS, 256), jnp.bfloat16),
            pltpu.VMEM((nblocks, SLICE_ROWS, KP), jnp.bfloat16),
            pltpu.SemaphoreType.DMA((nblocks,)),
            pltpu.SemaphoreType.DMA((nblocks,)),
        ],
        compiler_params=pltpu.CompilerParams(vmem_limit_bytes=40 * MIB),
        cost_estimate=pl.CostEstimate(flops=0, bytes_accessed=rows * 11264, transcendentals=0),
    )(orb, pair, panel, amp)


def ladder_kernel(own, other, integrals, recv, a, b, prod, load_sem, give_sem, get_sem, send_sem, recv_sem, self_sem):
    v = lax.axis_index("vv")
    g = lax.axis_index("grp")
    h = 1 - g
    flip = v + 2 - 4 * lax.rem(v // 2, 2)
    load_b = pltpu.make_async_copy(integrals.at[0], b, load_sem.at[0])
    load_a = pltpu.make_async_copy(own, a.at[pl.ds(g * HALF, HALF)], load_sem.at[1])
    load_a.start()
    load_b.start()

    barrier = pltpu.get_barrier_semaphore()

    @pl.loop(1, N_VV)
    def _(k):
        pl.semaphore_signal(barrier, inc=1, device_id=(lax.rem(v + k, N_VV), g), device_id_type=MESH)

    pl.semaphore_signal(barrier, inc=1, device_id=(v, h), device_id_type=MESH)
    pl.semaphore_signal(barrier, inc=1, device_id=(flip, h), device_id_type=MESH)
    pl.semaphore_wait(barrier, N_VV + 1)

    n_chunks = HALF // 2 // CHUNK

    def gives(j):
        first = pltpu.make_async_remote_copy(
            src_ref=own.at[pl.ds(j * CHUNK, CHUNK)],
            dst_ref=a.at[pl.ds(g * HALF + j * CHUNK, CHUNK)],
            send_sem=give_sem,
            recv_sem=get_sem.at[j],
            device_id=(v, h),
            device_id_type=MESH,
        )
        second = pltpu.make_async_remote_copy(
            src_ref=other.at[pl.ds(j * CHUNK, CHUNK)],
            dst_ref=a.at[pl.ds(g * HALF + HALF // 2 + j * CHUNK, CHUNK)],
            send_sem=give_sem,
            recv_sem=get_sem.at[n_chunks + j],
            device_id=(flip, h),
            device_id_type=MESH,
        )
        return first, second

    for j in range(n_chunks):
        for c in gives(j):
            c.start()
    load_a.wait()
    load_b.wait()

    rot = lax.rem(v // 8, 4)

    @pl.loop(0, IJ // BLOCK)
    def _(i):
        part = i // 4
        half = lax.rem(g + part, 2)
        q = lax.rem(i + rot, 4)

        @pl.when(part == 1)
        def _():
            for s in range(BLOCK // CHUNK):
                idx = q * (BLOCK // CHUNK) + s
                here = a.at[pl.ds(h * HALF + idx * CHUNK, CHUNK)]
                pltpu.make_async_remote_copy(here, here, give_sem, get_sem.at[idx], device_id=(v, h), device_id_type=MESH).wait_recv()

        row = pl.multiple_of(half * HALF + q * BLOCK, BLOCK)
        w0 = half * (N_VV // 2) + q * PER_BLOCK

        @pl.loop(0, ROWS // NCOL)
        def _(n):
            col = pl.multiple_of(n * NCOL, NCOL)
            y = lax.dot_general(
                a[pl.ds(row, BLOCK), :],
                b[pl.ds(col, NCOL), :],
                (((1,), (1,)), ((), ())),
                preferred_element_type=jnp.float32,
            )
            prod[pl.ds(w0, PER_BLOCK), :, pl.ds(col, NCOL)] = y.astype(jnp.bfloat16).reshape(PER_BLOCK, OWN, NCOL)

        @pl.loop(0, PER_BLOCK)
        def _(t):
            w = w0 + lax.rem(t + v, PER_BLOCK)

            @pl.when(w == v)
            def _():
                pltpu.make_async_copy(prod.at[v], recv.at[v], self_sem).start()

            @pl.when(w != v)
            def _():
                pltpu.make_async_remote_copy(
                    src_ref=prod.at[w],
                    dst_ref=recv.at[v],
                    send_sem=send_sem,
                    recv_sem=recv_sem,
                    device_id=(w, g),
                    device_id_type=MESH,
                ).start()

    for j in range(n_chunks):
        for c in gives(j):
            c.wait_send()
    pltpu.make_async_copy(prod.at[v], recv.at[v], self_sem).wait()
    rest = pltpu.make_async_remote_copy(
        src_ref=prod.at[pl.ds(0, N_VV - 1)],
        dst_ref=recv.at[pl.ds(0, N_VV - 1)],
        send_sem=send_sem,
        recv_sem=recv_sem,
        device_id=(v, h),
        device_id_type=MESH,
    )
    rest.wait_send()
    rest.wait_recv()


def ladder(own, other, integrals):
    hbm = pl.BlockSpec(memory_space=pl.ANY)
    return pl.pallas_call(
        ladder_kernel,
        name="ladder",
        out_shape=jax.ShapeDtypeStruct((N_VV, OWN, ROWS), jnp.bfloat16),
        in_specs=[hbm] * 3,
        out_specs=hbm,
        scratch_shapes=[
            pltpu.VMEM((IJ, KP), jnp.bfloat16),
            pltpu.VMEM((ROWS, KP), jnp.bfloat16),
            pltpu.VMEM((N_VV, OWN, ROWS), jnp.bfloat16),
            pltpu.SemaphoreType.DMA((2,)),
            pltpu.SemaphoreType.DMA,
            pltpu.SemaphoreType.DMA((HALF // CHUNK,)),
            pltpu.SemaphoreType.DMA,
            pltpu.SemaphoreType.DMA,
            pltpu.SemaphoreType.DMA,
        ],
        compiler_params=pltpu.CompilerParams(
            collective_id=0, has_side_effects=True, vmem_limit_bytes=48 * MIB
        ),
        cost_estimate=pl.CostEstimate(flops=2 * IJ * ROWS * KP, bytes_accessed=40 * MIB, transcendentals=0),
    )(own, other, integrals)


TCOL = 256


def swap_kernel(x, out):
    row = lax.broadcasted_iota(jnp.int32, (256, 256), 0)
    col = lax.broadcasted_iota(jnp.int32, (256, 256), 1)
    perm = jnp.where(lax.rem(row, 16) * 16 + row // 16 == col, 1.0, 0.0).astype(jnp.bfloat16)
    for i in range(OWN // 16):
        for s in range(N_VV // 16):
            block = x[pl.ds(s * 16, 16), pl.ds(i * 16, 16), :].reshape(256, TCOL)
            y = jnp.dot(perm, block, preferred_element_type=jnp.float32)
            out[pl.ds(i * 16, 16), pl.ds(s * 16, 16), :] = y.astype(jnp.bfloat16).reshape(16, 16, TCOL)


def swap(x):
    return pl.pallas_call(
        swap_kernel,
        name="swap",
        grid=(ROWS // TCOL,),
        out_shape=jax.ShapeDtypeStruct((OWN, N_VV, ROWS), jnp.bfloat16),
        in_specs=[pl.BlockSpec((N_VV, OWN, TCOL), lambda i: (0, 0, i))],
        out_specs=pl.BlockSpec((OWN, N_VV, TCOL), lambda i: (0, 0, i)),
        compiler_params=pltpu.CompilerParams(vmem_limit_bytes=32 * MIB),
        cost_estimate=pl.CostEstimate(flops=0, bytes_accessed=2 * IJ * ROWS * 2, transcendentals=0),
    )(x)


def shards(integrals, amplitudes, orbital_irrep, pair_irrep, panel_block):
    flipped = [(i, i ^ 2) for i in range(N_VV)]
    other_irrep = lax.ppermute(pair_irrep, "vv", flipped)
    own = slice_block(0, HALF, orbital_irrep, pair_irrep, panel_block, amplitudes)
    other = slice_block(HALF // 2, HALF // 2, orbital_irrep, other_irrep, panel_block, amplitudes)
    return swap(ladder(own, other, integrals))


def solution(mesh):
    return jax.shard_map(
        shards,
        mesh=mesh,
        in_specs=(P("vv", "grp", None), P("grp", None), P(), P("vv"), P()),
        out_specs=P("vv", None, "grp"),
        check_vma=False,
    )
```

time: 378 us -> 208 us (0.55)
  the two profiles are of different devices: /device:TPU:1 before, /device:TPU:35 now
where the time goes in v1:
time: 208 us; the launch traced here: 207 us
  Pallas kernels  200 us (96%)
  local copies, waits for them, and re-layouts  4.35 us (2%)
    pallas_call x1, Pallas kernels, ladder(): pl.pallas_call(ladder_kernel, name='ladder', out_shape=jax.ShapeDtypeStru...  181 us
    pallas_call x2, Pallas kernels, slice_block(): pl.pallas_call(functools.partial(slice_kernel, row0, nblocks), name='slic...  11.6 us
    pallas_call x1, Pallas kernels, swap(): pl.pallas_call(swap_kernel, name='swap', grid=(ROWS // TCOL,), out_shape=...  7.41 us
    unnamed x4, local copies, waits for them, and re-layouts  4.35 us
  transfers between devices with their start and end apart: 1, of which 0 were waited for; matrix products, arithmetic and copies ran while one was open for 0% of the time, Pallas kernels for 3%

profile of v1, /device:TPU:35, one launch (start us, length us, event | category | flops | bytes accessed | tf_op | source)
XLA Modules:
  0.0 207.5 jit_solution(15884934782820869272)
XLA Ops:
  0.0 1.8 collective-permute-start
  3.2 0.0 copy-start.1
  3.2 0.7 copy-done.1
  3.9 6.5 %slice_block.2.own = bf16[1024,1536]{1,0:T(8,128)(2,1)S(1)} custom-call(s32[768]{0:T(1024)S(1)} %copy-done.1, s32[1]{0:T(128)S(6)} %copy.6.pair, s32[1]{0:T(128)S(6)} %copy.7.panel, bf16[1024,12288]{1,0:T(8,128)(2,1)} %amp.3), custom_call_target="tpu_custom_call" | custom-call | bytes 11534336 | tf_op jit(solution)/shard_map/slice_block/pallas_call | solution.py:77
  10.4 0.0 collective-permute-done.pair
  10.4 5.0 %slice_block.3.other = bf16[512,1536]{1,0:T(8,128)(2,1)S(1)} custom-call(s32[768]{0:T(1024)S(1)} %copy-done.1, s32[1]{0:T(128)} %collective-permute-done.pair, s32[1]{0:T(128)S(6)} %copy.7.panel, bf16[1024,12288]{1,0:T(8,128)(2,1)} %amp.3), custom_call_target="tpu_custom_call" | custom-call | bytes 5767168 | tf_op jit(solution)/shard_map/slice_block/pallas_call | solution.py:77
  15.5 180.9 %ladder.1.x = bf16[64,32,2304]{2,1,0:T(8,128)(2,1)} custom-call(bf16[1024,1536]{1,0:T(8,128)(2,1)S(1)} %slice_block.2.own, bf16[512,1536]{1,0:T(8,128)(2,1)S(1)} %slice_block.3.other, bf16[1,2304,1536]{2,1,0:T(8,128)(2,1)} %integrals.1), custom_call_target="tpu_custom_call" | custom-call | flops 14495514624 | bytes 41943040 | tf_op jit(solution)/shard_map/ladder/pallas_call | solution.py:207
  196.4 0.0 copy-start
  196.4 3.7 %copy-done = bf16[64,32,2304]{2,1,0:T(8,128)(2,1)S(1)} copy-done((bf16[64,32,2304]{2,1,0:T(8,128)(2,1)S(1)}, bf16[64,32,2304]{2,1,0:T(8,128)(2,1)}, u32[]{:S(2)}) %copy-start) | copy-done | bytes 9437208
  200.1 7.4 %swap.1 = bf16[32,64,2304]{2,1,0:T(8,128)(2,1)} custom-call(bf16[64,32,2304]{2,1,0:T(8,128)(2,1)S(1)} %copy-done), custom_call_target="tpu_custom_call" | custom-call | bytes 18874368 | tf_op jit(solution)/shard_map/swap/pallas_call | solution.py:246
Async XLA Ops:
  0.0 10.4 %collective-permute-start = (s32[1]{0:T(128)}, s32[1]{0:T(128)}, u32[]{:S(2)}, u32[]{:S(2)}) collective-permute-start(s32[1]{0:T(128)} %param.8), channel_id=1, source_target_pairs={{0,4},{2,6},{4,0},{6,2},{8,12},{10,14},{12,8},{14,10},{16,20},{18,... | collective-permute-start | bytes 20 | tf_op jit(solution)/shard_map/ppermute | solution.py:260
  3.2 0.7 copy-start.1
  196.4 3.7 %copy-start = (bf16[64,32,2304]{2,1,0:T(8,128)(2,1)S(1)}, bf16[64,32,2304]{2,1,0:T(8,128)(2,1)}, u32[]{:S(2)}) copy-start(bf16[64,32,2304]{2,1,0:T(8,128)(2,1)} %ladder.1.x) | copy-start | bytes 28311556

commit v2 on v1

v2 whole, which is shorter than its diff:
```python
import functools

import jax
import jax.numpy as jnp
from jax import lax
from jax.experimental import pallas as pl
from jax.experimental.pallas import tpu as pltpu
from jax.sharding import PartitionSpec as P

NIRR = 8
BS = 96
DW = 16
NV = NIRR * BS
KP = DW * BS
ROWS = 2304
IJ = 2048
HALF = IJ // 2
N_VV = 64
OWN = IJ // N_VV
CHUNK = 128
WINDOW = 3
MESH = pl.DeviceIdType.MESH
SLICE_ROWS = 512
SUB_ROWS = 128
MIB = 1024 * 1024


def slice_kernel(row0, nblocks, orb, pair, panel, amp, out, win, outbuf, in_sem, out_sem):
    target = pair[0] ^ orb[panel[0] * BS]
    allowed = jnp.int32(0)
    for k in range(NIRR):
        allowed += jnp.where(orb[k * BS] == target, jnp.int32(k), jnp.int32(0))
    tile = jnp.minimum(allowed * BS // 128, 4)
    off = allowed * BS - tile * 128
    units = [(b, q) for b in range(nblocks) for q in range(DW // 4)]

    def window(b, q, j):
        d = q * 4 + j
        return pltpu.make_async_copy(
            amp.at[pl.ds(row0 + b * SLICE_ROWS, SLICE_ROWS), pl.ds(pl.multiple_of(d * NV + tile * 128, 128), 256)],
            win.at[d, pl.ds(b * SLICE_ROWS, SLICE_ROWS)],
            in_sem.at[b, q],
        )

    def result(b, q):
        part = (pl.ds(b * SLICE_ROWS, SLICE_ROWS), pl.ds(q * 4 * BS, 4 * BS))
        return pltpu.make_async_copy(outbuf.at[part], out.at[part], out_sem.at[b, q])

    for b, q in units:
        for j in range(4):
            window(b, q, j).start()
    lane = lax.broadcasted_iota(jnp.int32, (SUB_ROWS, 128), 1)

    for b, q in units:
        for j in range(4):
            window(b, q, j).wait()

        @pl.loop(0, SLICE_ROWS // SUB_ROWS)
        def _(r):
            rows = pl.ds(pl.multiple_of(b * SLICE_ROWS + r * SUB_ROWS, SUB_ROWS), SUB_ROWS)
            w = [
                pltpu.roll(win[q * 4 + j, rows].astype(jnp.float32), lax.rem((96 * j) % 128 - off + 512, 256), 1)
                for j in range(4)
            ]
            t0 = jnp.where(lane < 96, w[0][:, :128], w[1][:, :128])
            t1 = jnp.where(lane < 64, w[1][:, 128:], w[2][:, :128])
            t2 = jnp.where(lane < 32, w[2][:, 128:], w[3][:, :128])
            outbuf[rows, q * 384 : (q + 1) * 384] = jnp.concatenate([t0, t1, t2], axis=1).astype(jnp.bfloat16)

        result(b, q).start()
    for b, q in units:
        result(b, q).wait()


def slice_block(row0, rows, orb, pair, panel, amp):
    nblocks = rows // SLICE_ROWS
    smem = pl.BlockSpec(memory_space=pltpu.SMEM)
    hbm = pl.BlockSpec(memory_space=pl.ANY)
    return pl.pallas_call(
        functools.partial(slice_kernel, row0, nblocks),
        name="slice_block",
        out_shape=jax.ShapeDtypeStruct((rows, KP), jnp.bfloat16),
        in_specs=[smem, smem, smem, hbm],
        out_specs=hbm,
        scratch_shapes=[
            pltpu.VMEM((DW, rows, 256), jnp.bfloat16),
            pltpu.VMEM((rows, KP), jnp.bfloat16),
            pltpu.SemaphoreType.DMA((nblocks, DW // 4)),
            pltpu.SemaphoreType.DMA((nblocks, DW // 4)),
        ],
        compiler_params=pltpu.CompilerParams(vmem_limit_bytes=44 * MIB),
        cost_estimate=pl.CostEstimate(flops=0, bytes_accessed=rows * 11264, transcendentals=0),
    )(orb, pair, panel, amp)


def ladder_kernel(own, other, integrals, recv, a, b, prod, stage, load_sem, give_sem, get_sem, send_sem, recv_sem, self_sem, x_send, x_recv):
    v = lax.axis_index("vv")
    g = lax.axis_index("grp")
    h = 1 - g
    z, y = v // 16, lax.rem(v // 4, 4)
    xh, c = lax.rem(v // 2, 2), lax.rem(v, 2)
    flip = v + 2 - 4 * xh
    turn = 1 - 2 * c
    load_b = pltpu.make_async_copy(integrals.at[0], b, load_sem.at[0])
    load_a = pltpu.make_async_copy(own, a.at[pl.ds(g * HALF, HALF)], load_sem.at[1])
    load_a.start()
    load_b.start()

    barrier = pltpu.get_barrier_semaphore()

    def greet(w, group):
        pl.semaphore_signal(barrier, inc=1, device_id=(w, group), device_id_type=MESH)

    greet(flip, g)
    greet(v, h)
    greet(flip, h)

    @pl.loop(1, N_VV // 2)
    def _(k):
        p = lax.rem(v // 4 * 2 + c + k, N_VV // 2)
        greet(p // 2 * 4 + xh * 2 + lax.rem(p, 2), g)

    pl.semaphore_wait(barrier, N_VV // 2 + 2)

    n_chunks = HALF // 2 // CHUNK

    def gives(j):
        first = pltpu.make_async_remote_copy(
            src_ref=own.at[pl.ds(j * CHUNK, CHUNK)],
            dst_ref=a.at[pl.ds(g * HALF + j * CHUNK, CHUNK)],
            send_sem=give_sem,
            recv_sem=get_sem.at[j],
            device_id=(v, h),
            device_id_type=MESH,
        )
        second = pltpu.make_async_remote_copy(
            src_ref=other.at[pl.ds(j * CHUNK, CHUNK)],
            dst_ref=a.at[pl.ds(g * HALF + HALF // 2 + j * CHUNK, CHUNK)],
            send_sem=give_sem,
            recv_sem=get_sem.at[n_chunks + j],
            device_id=(flip, h),
            device_id_type=MESH,
        )
        return first, second

    for j in range(n_chunks):
        for copy in gives(lax.rem(y + turn * j + 4, 4)):
            copy.start()
    load_a.wait()
    load_b.wait()

    def multiply(row, w0, rows, cols):
        @pl.loop(0, ROWS // cols)
        def _(n):
            col = pl.multiple_of(n * cols, cols)
            part = lax.dot_general(
                a[pl.ds(pl.multiple_of(row, rows), rows), :],
                b[pl.ds(col, cols), :],
                (((1,), (1,)), ((), ())),
                preferred_element_type=jnp.float32,
            )
            prod[pl.ds(w0, rows // OWN), :, pl.ds(col, cols)] = part.astype(jnp.bfloat16).reshape(rows // OWN, OWN, cols)

    def push(source, w, sender):
        @pl.when(w == v)
        def _():
            pltpu.make_async_copy(source, recv.at[sender], self_sem).start()

        @pl.when(w != v)
        def _():
            pltpu.make_async_remote_copy(
                src_ref=source,
                dst_ref=recv.at[sender],
                send_sem=send_sem,
                recv_sem=recv_sem,
                device_id=(w, g),
                device_id_type=MESH,
            ).start()

    def near(q):
        @pl.loop(0, 2)
        def _(t):
            w = q * 4 + xh * 2 + lax.rem(c + t + 1, 2)
            push(prod.at[w], w, v)

    def across(q):
        return pltpu.make_async_remote_copy(
            src_ref=prod.at[pl.ds(q * 4 + 2 - xh * 2, 2)],
            dst_ref=stage.at[pl.ds(q * 2, 2)],
            send_sem=x_send.at[q],
            recv_sem=x_recv.at[q],
            device_id=(flip, g),
            device_id_type=MESH,
        )

    def forward(q):
        across(q).wait_recv()

        @pl.loop(0, 2)
        def _(t):
            core = lax.rem(c + t + 1, 2)
            push(stage.at[q * 2 + core], q * 4 + xh * 2 + core, flip)

    def crossing(k):
        i = k // 2
        half = jnp.where(lax.rem(k, 2) == 0, g, h)
        n = lax.rem(i, 4)
        dy = jnp.where(n == 0, 2, jnp.where(n == 1, 1, jnp.where(n == 2, 3, 0)))
        return (2 * half + lax.rem(z + 1 + i // 4, 2)) * 4 + lax.rem(y + turn * dy + 4, 4)

    @pl.loop(0, 2)
    def _(i):
        zz = 2 * g + lax.rem(z + i, 2)
        multiply(zz * 512, zz * 16, 512, 768)

        @pl.loop(0, 4)
        def _(j):
            near(zz * 4 + lax.rem(y + turn * j + 4, 4))

    @pl.loop(0, HALF // CHUNK)
    def _(i):
        q = (2 * h + lax.rem(i + z, 2)) * 4 + lax.rem(y + turn * (i // 2) + 4, 4)
        here = a.at[pl.ds(q * CHUNK, CHUNK)]
        pltpu.make_async_remote_copy(here, here, give_sem, get_sem.at[q - 8 * h], device_id=(v, h), device_id_type=MESH).wait_recv()
        multiply(q * CHUNK, q * 4, CHUNK, ROWS)
        near(q)

        @pl.when(i == 6)
        def _():
            across(crossing(0)).start()

    @pl.loop(1, WINDOW)
    def _(k):
        across(crossing(k)).start()

    @pl.loop(0, 16)
    def _(k):
        forward(crossing(k))

        @pl.when(k + WINDOW < 16)
        def _():
            across(crossing(k + WINDOW)).start()

    for j in range(n_chunks):
        for copy in gives(j):
            copy.wait_send()

    @pl.loop(0, 16)
    def _(q):
        across(q).wait_send()

    pltpu.make_async_copy(prod.at[pl.ds(0, 2)], recv.at[pl.ds(0, 2)], self_sem).wait()
    rest = pltpu.make_async_remote_copy(
        src_ref=prod.at[pl.ds(0, N_VV - 2)],
        dst_ref=recv.at[pl.ds(0, N_VV - 2)],
        send_sem=send_sem,
        recv_sem=recv_sem,
        device_id=(flip, g),
        device_id_type=MESH,
    )
    rest.wait_send()
    rest.wait_recv()


def ladder(own, other, integrals):
    hbm = pl.BlockSpec(memory_space=pl.ANY)
    return pl.pallas_call(
        ladder_kernel,
        name="ladder",
        out_shape=pltpu.VMEM((N_VV, OWN, ROWS), jnp.bfloat16),
        in_specs=[hbm] * 3,
        out_specs=pl.BlockSpec(memory_space=pltpu.VMEM),
        scratch_shapes=[
            pltpu.VMEM((IJ, KP), jnp.bfloat16),
            pltpu.VMEM((ROWS, KP), jnp.bfloat16),
            pltpu.VMEM((N_VV, OWN, ROWS), jnp.bfloat16),
            pltpu.VMEM((N_VV // 2, OWN, ROWS), jnp.bfloat16),
            pltpu.SemaphoreType.DMA((2,)),
            pltpu.SemaphoreType.DMA,
            pltpu.SemaphoreType.DMA((HALF // CHUNK,)),
            pltpu.SemaphoreType.DMA,
            pltpu.SemaphoreType.DMA,
            pltpu.SemaphoreType.DMA,
            pltpu.SemaphoreType.DMA((16,)),
            pltpu.SemaphoreType.DMA((16,)),
        ],
        compiler_params=pltpu.CompilerParams(
            collective_id=0, has_side_effects=True, vmem_limit_bytes=40 * MIB
        ),
        cost_estimate=pl.CostEstimate(flops=2 * IJ * ROWS * KP, bytes_accessed=40 * MIB, transcendentals=0),
    )(own, other, integrals)


TCOL = 768


def swap_kernel(x, out, buf, sem):
    row = lax.broadcasted_iota(jnp.int32, (256, 256), 0)
    col = lax.broadcasted_iota(jnp.int32, (256, 256), 1)
    perm = jnp.where(lax.rem(row, 16) * 16 + row // 16 == col, 1.0, 0.0).astype(jnp.bfloat16)

    def result(i, n):
        part = (pl.ds(i * 16, 16), slice(None), pl.ds(n * TCOL, TCOL))
        return pltpu.make_async_copy(buf.at[part], out.at[part], sem.at[i, n])

    for i in range(OWN // 16):
        for n in range(ROWS // TCOL):
            for s in range(N_VV // 16):
                block = x[pl.ds(s * 16, 16), pl.ds(i * 16, 16), pl.ds(n * TCOL, TCOL)].reshape(256, TCOL)
                part = jnp.dot(perm, block, preferred_element_type=jnp.float32)
                buf[pl.ds(i * 16, 16), pl.ds(s * 16, 16), pl.ds(n * TCOL, TCOL)] = part.astype(jnp.bfloat16).reshape(16, 16, TCOL)
            result(i, n).start()
    for i in range(OWN // 16):
        for n in range(ROWS // TCOL):
            result(i, n).wait()


def swap(x):
    return pl.pallas_call(
        swap_kernel,
        name="swap",
        out_shape=jax.ShapeDtypeStruct((OWN, N_VV, ROWS), jnp.bfloat16),
        in_specs=[pl.BlockSpec(memory_space=pltpu.VMEM)],
        out_specs=pl.BlockSpec(memory_space=pl.ANY),
        scratch_shapes=[
            pltpu.VMEM((OWN, N_VV, ROWS), jnp.bfloat16),
            pltpu.SemaphoreType.DMA((OWN // 16, ROWS // TCOL)),
        ],
        compiler_params=pltpu.CompilerParams(vmem_limit_bytes=24 * MIB),
        cost_estimate=pl.CostEstimate(flops=0, bytes_accessed=2 * IJ * ROWS * 2, transcendentals=0),
    )(x)


def shards(integrals, amplitudes, orbital_irrep, pair_irrep, panel_block):
    flipped = [(i, i ^ 2) for i in range(N_VV)]
    other_irrep = lax.ppermute(pair_irrep, "vv", flipped)
    own = slice_block(0, HALF, orbital_irrep, pair_irrep, panel_block, amplitudes)
    other = slice_block(HALF // 2, HALF // 2, orbital_irrep, other_irrep, panel_block, amplitudes)
    return swap(ladder(own, other, integrals))


def solution(mesh):
    return jax.shard_map(
        shards,
        mesh=mesh,
        in_specs=(P("vv", "grp", None), P("grp", None), P(), P("vv"), P()),
        out_specs=P("vv", None, "grp"),
        check_vma=False,
    )
```

time: 208 us -> 178 us (0.86)
  the two profiles are of different devices: /device:TPU:35 before, /device:TPU:1 now
where the time goes in v2:
time: 178 us; the launch traced here: 175 us
  Pallas kernels  170 us (96%)
  starting transfers between devices  3.57 us (2%)
    pallas_call x1, Pallas kernels, ladder(): pl.pallas_call(ladder_kernel, name='ladder', out_shape=pltpu.VMEM((N_VV,...  154 us
    pallas_call x2, Pallas kernels, slice_block(): pl.pallas_call(functools.partial(slice_kernel, row0, nblocks), name='slic...  12 us
    pallas_call x1, Pallas kernels, swap(): pl.pallas_call(swap_kernel, name='swap', out_shape=jax.ShapeDtypeStruct((...  4.27 us
    ppermute x1, starting transfers between devices, shards(): other_irrep = lax.ppermute(pair_irrep, 'vv', flipped)  3.57 us
  transfers between devices with their start and end apart: 1, of which 0 were waited for; matrix products, arithmetic and copies ran while one was open for 0% of the time, Pallas kernels for 4%

profile of v2, /device:TPU:1, one launch (start us, length us, event | category | flops | bytes accessed | tf_op | source)
XLA Modules:
  0.0 175.4 jit_solution(14764088307444257733)
XLA Ops:
  0.0 3.6 %collective-permute-start = (s32[1]{0:T(128)}, s32[1]{0:T(128)}, u32[]{:S(2)}, u32[]{:S(2)}) collective-permute-start(s32[1]{0:T(128)} %param.8), channel_id=1, source_target_pairs={{0,4},{2,6},{4,0},{6,2},{8,12},{10,14},{12,8},{14,10},{16,20},{18,... | collective-permute-start | bytes 20 | tf_op jit(solution)/shard_map/ppermute | solution.py:336
  4.9 0.0 copy-start
  4.9 0.7 copy-done
  5.6 7.0 %slice_block.2.own = bf16[1024,1536]{1,0:T(8,128)(2,1)S(1)} custom-call(s32[768]{0:T(1024)S(1)} %copy-done, s32[1]{0:T(128)S(6)} %copy.6.pair, s32[1]{0:T(128)S(6)} %copy.7.panel, bf16[1024,12288]{1,0:T(8,128)(2,1)} %amp.3), custom_call_target="tpu_custom_call" | custom-call | bytes 11534336 | tf_op jit(solution)/shard_map/slice_block/pallas_call | solution.py:79
  12.6 0.0 collective-permute-done.pair
  12.6 5.0 %slice_block.3.other = bf16[512,1536]{1,0:T(8,128)(2,1)S(1)} custom-call(s32[768]{0:T(1024)S(1)} %copy-done, s32[1]{0:T(128)} %collective-permute-done.pair, s32[1]{0:T(128)S(6)} %copy.7.panel, bf16[1024,12288]{1,0:T(8,128)(2,1)} %amp.3), custom_call_target="tpu_custom_call" | custom-call | bytes 5767168 | tf_op jit(solution)/shard_map/slice_block/pallas_call | solution.py:79
  17.6 153.5 %ladder.1.x = bf16[64,32,2304]{2,1,0:T(8,128)(2,1)S(1)} custom-call(bf16[1024,1536]{1,0:T(8,128)(2,1)S(1)} %slice_block.2.own, bf16[512,1536]{1,0:T(8,128)(2,1)S(1)} %slice_block.3.other, bf16[1,2304,1536]{2,1,0:T(8,128)(2,1)} %integrals.1), custom_call_target="tpu_custom_call" | custom-call | flops 14495514624 | bytes 41943040 | tf_op jit(solution)/shard_map/ladder/pallas_call | solution.py:267
  171.1 4.3 %swap.1 = bf16[32,64,2304]{2,1,0:T(8,128)(2,1)} custom-call(bf16[64,32,2304]{2,1,0:T(8,128)(2,1)S(1)} %ladder.1.x), custom_call_target="tpu_custom_call" | custom-call | bytes 18874368 | tf_op jit(solution)/shard_map/swap/pallas_call | solution.py:319
Async XLA Ops:
  0.0 12.6 %collective-permute-start = (s32[1]{0:T(128)}, s32[1]{0:T(128)}, u32[]{:S(2)}, u32[]{:S(2)}) collective-permute-start(s32[1]{0:T(128)} %param.8), channel_id=1, source_target_pairs={{0,4},{2,6},{4,0},{6,2},{8,12},{10,14},{12,8},{14,10},{16,20},{18,... | collective-permute-start | bytes 20 | tf_op jit(solution)/shard_map/ppermute | solution.py:336
  4.9 0.7 copy-start

commit v3 on v2

--- a/solution.py
+++ b/solution.py
@@ -20,44 +20,53 @@
 CHUNK = 128
 WINDOW = 3
 MESH = pl.DeviceIdType.MESH
-SLICE_ROWS = 512
-SUB_ROWS = 128
+PART = HALF // 2
+SUB_ROWS = 256
 MIB = 1024 * 1024
 
 
-def slice_kernel(row0, nblocks, orb, pair, panel, amp, out, win, outbuf, in_sem, out_sem):
-    target = pair[0] ^ orb[panel[0] * BS]
-    allowed = jnp.int32(0)
-    for k in range(NIRR):
-        allowed += jnp.where(orb[k * BS] == target, jnp.int32(k), jnp.int32(0))
-    tile = jnp.minimum(allowed * BS // 128, 4)
-    off = allowed * BS - tile * 128
-    units = [(b, q) for b in range(nblocks) for q in range(DW // 4)]
-
-    def window(b, q, j):
+def slice_kernel(labels, pair, other_pair, panel, amp, own, other, win, buf, in_sem, out_sem):
+    panel_irrep = labels[panel[0] * BS]
+
+    def place(irrep):
+        target = irrep ^ panel_irrep
+        allowed = jnp.int32(0)
+        for k in range(NIRR):
+            allowed += jnp.where(labels[k * BS] == target, jnp.int32(k), jnp.int32(0))
+        tile = jnp.minimum(allowed * BS // 128, 4)
+        return tile, allowed * BS - tile * 128
+
+    mine, theirs = place(pair[0]), place(other_pair[0])
+    parts = [(mine, 0, own, 0), (theirs, HALF // 2, other, 0), (mine, HALF // 2, own, HALF // 2)]
+    units = [(p, q) for p in range(3) for q in range(DW // 4)]
+
+    def window(p, q, j):
+        (tile, _), row, _, _ = parts[p]
         d = q * 4 + j
         return pltpu.make_async_copy(
-            amp.at[pl.ds(row0 + b * SLICE_ROWS, SLICE_ROWS), pl.ds(pl.multiple_of(d * NV + tile * 128, 128), 256)],
-            win.at[d, pl.ds(b * SLICE_ROWS, SLICE_ROWS)],
-            in_sem.at[b, q],
+            amp.at[pl.ds(row, PART), pl.ds(pl.multiple_of(d * NV + tile * 128, 128), 256)],
+            win.at[d, pl.ds(p * PART, PART)],
+            in_sem.at[p, q],
         )
 
-    def result(b, q):
-        part = (pl.ds(b * SLICE_ROWS, SLICE_ROWS), pl.ds(q * 4 * BS, 4 * BS))
-        return pltpu.make_async_copy(outbuf.at[part], out.at[part], out_sem.at[b, q])
-
-    for b, q in units:
+    def result(p, q):
+        _, _, out, row = parts[p]
+        cols = pl.ds(q * 4 * BS, 4 * BS)
+        return pltpu.make_async_copy(buf.at[pl.ds(p * PART, PART), cols], out.at[pl.ds(row, PART), cols], out_sem.at[p, q])
+
+    for p, q in units:
         for j in range(4):
-            window(b, q, j).start()
+            window(p, q, j).start()
     lane = lax.broadcasted_iota(jnp.int32, (SUB_ROWS, 128), 1)
 
-    for b, q in units:
+    for p, q in units:
+        off = parts[p][0][1]
         for j in range(4):
-            window(b, q, j).wait()
-
-        @pl.loop(0, SLICE_ROWS // SUB_ROWS)
+            window(p, q, j).wait()
+
+        @pl.loop(0, PART // SUB_ROWS)
         def _(r):
-            rows = pl.ds(pl.multiple_of(b * SLICE_ROWS + r * SUB_ROWS, SUB_ROWS), SUB_ROWS)
+            rows = pl.ds(pl.multiple_of(p * PART + r * SUB_ROWS, SUB_ROWS), SUB_ROWS)
             w = [
                 pltpu.roll(win[q * 4 + j, rows].astype(jnp.float32), lax.rem((96 * j) % 128 - off + 512, 256), 1)
                 for j in range(4)
@@ -65,32 +74,31 @@
             t0 = jnp.where(lane < 96, w[0][:, :128], w[1][:, :128])
             t1 = jnp.where(lane < 64, w[1][:, 128:], w[2][:, :128])
             t2 = jnp.where(lane < 32, w[2][:, 128:], w[3][:, :128])
-            outbuf[rows, q * 384 : (q + 1) * 384] = jnp.concatenate([t0, t1, t2], axis=1).astype(jnp.bfloat16)
-
-        result(b, q).start()
-    for b, q in units:
-        result(b, q).wait()
-
-
-def slice_block(row0, rows, orb, pair, panel, amp):
-    nblocks = rows // SLICE_ROWS
+            buf[rows, q * 384 : (q + 1) * 384] = jnp.concatenate([t0, t1, t2], axis=1).astype(jnp.bfloat16)
+
+        result(p, q).start()
+    for p, q in units:
+        result(p, q).wait()
+
+
+def slice_blocks(orb, pair, other_pair, panel, amp):
     smem = pl.BlockSpec(memory_space=pltpu.SMEM)
     hbm = pl.BlockSpec(memory_space=pl.ANY)
     return pl.pallas_call(
-        functools.partial(slice_kernel, row0, nblocks),
-        name="slice_block",
-        out_shape=jax.ShapeDtypeStruct((rows, KP), jnp.bfloat16),
-        in_specs=[smem, smem, smem, hbm],
-        out_specs=hbm,
+        slice_kernel,
+        name="slice_blocks",
+        out_shape=(jax.ShapeDtypeStruct((HALF, KP), jnp.bfloat16), jax.ShapeDtypeStruct((HALF // 2, KP), jnp.bfloat16)),
+        in_specs=[smem, smem, smem, smem, hbm],
+        out_specs=(hbm, hbm),
         scratch_shapes=[
-            pltpu.VMEM((DW, rows, 256), jnp.bfloat16),
-            pltpu.VMEM((rows, KP), jnp.bfloat16),
-            pltpu.SemaphoreType.DMA((nblocks, DW // 4)),
-            pltpu.SemaphoreType.DMA((nblocks, DW // 4)),
+            pltpu.VMEM((DW, 3 * PART, 256), jnp.bfloat16),
+            pltpu.VMEM((3 * PART, KP), jnp.bfloat16),
+            pltpu.SemaphoreType.DMA((3, DW // 4)),
+            pltpu.SemaphoreType.DMA((3, DW // 4)),
         ],
         compiler_params=pltpu.CompilerParams(vmem_limit_bytes=44 * MIB),
-        cost_estimate=pl.CostEstimate(flops=0, bytes_accessed=rows * 11264, transcendentals=0),
-    )(orb, pair, panel, amp)
+        cost_estimate=pl.CostEstimate(flops=0, bytes_accessed=3 * PART * 11264, transcendentals=0),
+    )(orb, pair, other_pair, panel, amp)
 
 
 def ladder_kernel(own, other, integrals, recv, a, b, prod, stage, load_sem, give_sem, get_sem, send_sem, recv_sem, self_sem, x_send, x_recv):
@@ -203,7 +211,7 @@
 
     def crossing(k):
         i = k // 2
-        half = jnp.where(lax.rem(k, 2) == 0, g, h)
+        half = lax.rem(z // 2 + k + 1, 2)
         n = lax.rem(i, 4)
         dy = jnp.where(n == 0, 2, jnp.where(n == 1, 1, jnp.where(n == 2, 3, 0)))
         return (2 * half + lax.rem(z + 1 + i // 4, 2)) * 4 + lax.rem(y + turn * dy + 4, 4)
@@ -334,8 +342,7 @@
 def shards(integrals, amplitudes, orbital_irrep, pair_irrep, panel_block):
     flipped = [(i, i ^ 2) for i in range(N_VV)]
     other_irrep = lax.ppermute(pair_irrep, "vv", flipped)
-    own = slice_block(0, HALF, orbital_irrep, pair_irrep, panel_block, amplitudes)
-    other = slice_block(HALF // 2, HALF // 2, orbital_irrep, other_irrep, panel_block, amplitudes)
+    own, other = slice_blocks(orbital_irrep, pair_irrep, other_irrep, panel_block, amplitudes)
     return swap(ladder(own, other, integrals))
 
 

time: 178 us -> 172 us (0.966); the launches traced: 175 us -> 172 us
  Pallas kernels: 170 us -> 166 us
    pallas_call x2 -> x1, Pallas kernels: 12 us -> 9.14 us  [slice_blocks(): pl.pallas_call(slice_kernel, name='slice_blocks', out_shape=(jax.ShapeDty...]
  transfers between devices with their start and end apart: 1 -> 1, of which waited for: 0 -> 0; matrix products, arithmetic and copies ran while one was open for 0% -> 0% of each run, Pallas kernels for 4% -> 0%
where the time goes in v3:
time: 172 us
  Pallas kernels  166 us (97%)
  starting transfers between devices  3.57 us (2%)
    pallas_call x1, Pallas kernels, ladder(): pl.pallas_call(ladder_kernel, name='ladder', out_shape=pltpu.VMEM((N_VV,...  153 us
    pallas_call x1, Pallas kernels, slice_blocks(): pl.pallas_call(slice_kernel, name='slice_blocks', out_shape=(jax.ShapeDty...  9.14 us
    pallas_call x1, Pallas kernels, swap(): pl.pallas_call(swap_kernel, name='swap', out_shape=jax.ShapeDtypeStruct((...  4.27 us
    ppermute x1, starting transfers between devices, shards(): other_irrep = lax.ppermute(pair_irrep, 'vv', flipped)  3.57 us
  transfers between devices with their start and end apart: 1, of which 0 were waited for; matrix products, arithmetic and copies ran while one was open for 0% of the time, Pallas kernels for 0%

profile of v3, /device:TPU:1, one launch (start us, length us, event | category | flops | bytes accessed | tf_op | source)
XLA Modules:
  0.0 172.1 jit_solution(9694305472417492829)
XLA Ops:
  0.0 3.6 %collective-permute-start = (s32[1]{0:T(128)}, s32[1]{0:T(128)}, u32[]{:S(2)}, u32[]{:S(2)}) collective-permute-start(s32[1]{0:T(128)} %param.8), channel_id=1, source_target_pairs={{0,4},{2,6},{4,0},{6,2},{8,12},{10,14},{12,8},{14,10},{16,20},{18,... | collective-permute-start | bytes 20 | tf_op jit(solution)/shard_map/ppermute | solution.py:344
  4.9 0.0 collective-permute-done.other_pair
  4.9 0.0 copy-start
  4.9 0.7 copy-done
  5.6 9.1 %slice_blocks.1 = (bf16[1024,1536]{1,0:T(8,128)(2,1)S(1)}, bf16[512,1536]{1,0:T(8,128)(2,1)S(1)}) custom-call(s32[768]{0:T(1024)S(1)} %copy-done, s32[1]{0:T(128)S(6)} %copy.6.pair, s32[1]{0:T(128)} %collective-permute-done.other_pair, s32[1]{0:T(128)S(6)} %copy.7.panel, bf16[1024,12288]{1,0:T(8,128)(2,1)} %amp.1), custom_call_target="tpu_custom_call" | custom-call | bytes 17301504 | tf_op jit(solution)/shard_map/slice_blocks/pallas_call | solution.py:87
  14.7 153.1 %ladder.1.x = bf16[64,32,2304]{2,1,0:T(8,128)(2,1)S(1)} custom-call(bf16[1024,1536]{1,0:T(8,128)(2,1)S(1)} %get-tuple-element.7.own, bf16[512,1536]{1,0:T(8,128)(2,1)S(1)} %get-tuple-element.8.other, bf16[1,2304,1536]{2,1,0:T(8,128)(2,1)} %integrals.1), custom_call_target="tpu_custom_call" | custom-call | flops 14495514624 | bytes 41943040 | tf_op jit(solution)/shard_map/ladder/pallas_call | solution.py:275
  167.8 4.3 %swap.1 = bf16[32,64,2304]{2,1,0:T(8,128)(2,1)} custom-call(bf16[64,32,2304]{2,1,0:T(8,128)(2,1)S(1)} %ladder.1.x), custom_call_target="tpu_custom_call" | custom-call | bytes 18874368 | tf_op jit(solution)/shard_map/swap/pallas_call | solution.py:327
Async XLA Ops:
  0.0 4.9 %collective-permute-start = (s32[1]{0:T(128)}, s32[1]{0:T(128)}, u32[]{:S(2)}, u32[]{:S(2)}) collective-permute-start(s32[1]{0:T(128)} %param.8), channel_id=1, source_target_pairs={{0,4},{2,6},{4,0},{6,2},{8,12},{10,14},{12,8},{14,10},{16,20},{18,... | collective-permute-start | bytes 20 | tf_op jit(solution)/shard_map/ppermute | solution.py:344
  4.9 0.7 copy-start

commit v4 on v3

--- a/solution.py
+++ b/solution.py
@@ -18,7 +18,8 @@
 N_VV = 64
 OWN = IJ // N_VV
 CHUNK = 128
-WINDOW = 3
+WINDOW = 4
+CROSS = N_VV // 2
 MESH = pl.DeviceIdType.MESH
 PART = HALF // 2
 SUB_ROWS = 256
@@ -191,30 +192,28 @@
             w = q * 4 + xh * 2 + lax.rem(c + t + 1, 2)
             push(prod.at[w], w, v)
 
-    def across(q):
-        return pltpu.make_async_remote_copy(
-            src_ref=prod.at[pl.ds(q * 4 + 2 - xh * 2, 2)],
-            dst_ref=stage.at[pl.ds(q * 2, 2)],
-            send_sem=x_send.at[q],
-            recv_sem=x_recv.at[q],
-            device_id=(flip, g),
-            device_id_type=MESH,
-        )
-
-    def forward(q):
-        across(q).wait_recv()
-
-        @pl.loop(0, 2)
-        def _(t):
-            core = lax.rem(c + t + 1, 2)
-            push(stage.at[q * 2 + core], q * 4 + xh * 2 + core, flip)
-
     def crossing(k):
         i = k // 2
         half = lax.rem(z // 2 + k + 1, 2)
         n = lax.rem(i, 4)
         dy = jnp.where(n == 0, 2, jnp.where(n == 1, 1, jnp.where(n == 2, 3, 0)))
         return (2 * half + lax.rem(z + 1 + i // 4, 2)) * 4 + lax.rem(y + turn * dy + 4, 4)
+
+    def across(u):
+        q, core = crossing(u // 2), lax.rem(c + u + 1, 2)
+        return pltpu.make_async_remote_copy(
+            src_ref=prod.at[q * 4 + 2 - xh * 2 + core],
+            dst_ref=stage.at[q * 2 + core],
+            send_sem=x_send.at[u],
+            recv_sem=x_recv.at[u],
+            device_id=(flip, g),
+            device_id_type=MESH,
+        )
+
+    def forward(u):
+        across(u).wait_recv()
+        q, core = crossing(u // 2), lax.rem(c + u + 1, 2)
+        push(stage.at[q * 2 + core], q * 4 + xh * 2 + core, flip)
 
     @pl.loop(0, 2)
     def _(i):
@@ -235,27 +234,28 @@
 
         @pl.when(i == 6)
         def _():
-            across(crossing(0)).start()
-
-    @pl.loop(1, WINDOW)
-    def _(k):
-        across(crossing(k)).start()
-
-    @pl.loop(0, 16)
-    def _(k):
-        forward(crossing(k))
-
-        @pl.when(k + WINDOW < 16)
+            across(0).start()
+            across(1).start()
+
+    @pl.loop(2, WINDOW)
+    def _(u):
+        across(u).start()
+
+    @pl.loop(0, CROSS)
+    def _(u):
+        forward(u)
+
+        @pl.when(u + WINDOW < CROSS)
         def _():
-            across(crossing(k + WINDOW)).start()
+            across(u + WINDOW).start()
 
     for j in range(n_chunks):
         for copy in gives(j):
             copy.wait_send()
 
-    @pl.loop(0, 16)
-    def _(q):
-        across(q).wait_send()
+    @pl.loop(0, CROSS)
+    def _(u):
+        across(u).wait_send()
 
     pltpu.make_async_copy(prod.at[pl.ds(0, 2)], recv.at[pl.ds(0, 2)], self_sem).wait()
     rest = pltpu.make_async_remote_copy(
@@ -289,8 +289,8 @@
             pltpu.SemaphoreType.DMA,
             pltpu.SemaphoreType.DMA,
             pltpu.SemaphoreType.DMA,
-            pltpu.SemaphoreType.DMA((16,)),
-            pltpu.SemaphoreType.DMA((16,)),
+            pltpu.SemaphoreType.DMA((CROSS,)),
+            pltpu.SemaphoreType.DMA((CROSS,)),
         ],
         compiler_params=pltpu.CompilerParams(
             collective_id=0, has_side_effects=True, vmem_limit_bytes=40 * MIB

time: 172 us -> 172 us (level)
  no operation moved by 1% of the time
where the time goes in v4:
time: 172 us; the launch traced here: 170 us
  Pallas kernels  165 us (96%)
  starting transfers between devices  3.57 us (2%)
    pallas_call x1, Pallas kernels, ladder(): pl.pallas_call(ladder_kernel, name='ladder', out_shape=pltpu.VMEM((N_VV,...  151 us
    pallas_call x1, Pallas kernels, slice_blocks(): pl.pallas_call(slice_kernel, name='slice_blocks', out_shape=(jax.ShapeDty...  9.14 us
    pallas_call x1, Pallas kernels, swap(): pl.pallas_call(swap_kernel, name='swap', out_shape=jax.ShapeDtypeStruct((...  4.27 us
    ppermute x1, starting transfers between devices, shards(): other_irrep = lax.ppermute(pair_irrep, 'vv', flipped)  3.57 us
  transfers between devices with their start and end apart: 1, of which 0 were waited for; matrix products, arithmetic and copies ran while one was open for 0% of the time, Pallas kernels for 0%

profile of v4, /device:TPU:1, one launch (start us, length us, event | category | flops | bytes accessed | tf_op | source)
XLA Modules:
  0.0 170.5 jit_solution(10543080859004173281)
XLA Ops:
  0.0 3.6 %collective-permute-start = (s32[1]{0:T(128)}, s32[1]{0:T(128)}, u32[]{:S(2)}, u32[]{:S(2)}) collective-permute-start(s32[1]{0:T(128)} %param.8), channel_id=1, source_target_pairs={{0,4},{2,6},{4,0},{6,2},{8,12},{10,14},{12,8},{14,10},{16,20},{18,... | collective-permute-start | bytes 20 | tf_op jit(solution)/shard_map/ppermute | solution.py:344
  4.9 0.0 collective-permute-done.other_pair
  4.9 0.0 copy-start
  4.9 0.7 copy-done
  5.6 9.1 %slice_blocks.1 = (bf16[1024,1536]{1,0:T(8,128)(2,1)S(1)}, bf16[512,1536]{1,0:T(8,128)(2,1)S(1)}) custom-call(s32[768]{0:T(1024)S(1)} %copy-done, s32[1]{0:T(128)S(6)} %copy.6.pair, s32[1]{0:T(128)} %collective-permute-done.other_pair, s32[1]{0:T(128)S(6)} %copy.7.panel, bf16[1024,12288]{1,0:T(8,128)(2,1)} %amp.1), custom_call_target="tpu_custom_call" | custom-call | bytes 17301504 | tf_op jit(solution)/shard_map/slice_blocks/pallas_call | solution.py:88
  14.7 151.5 %ladder.1.x = bf16[64,32,2304]{2,1,0:T(8,128)(2,1)S(1)} custom-call(bf16[1024,1536]{1,0:T(8,128)(2,1)S(1)} %get-tuple-element.7.own, bf16[512,1536]{1,0:T(8,128)(2,1)S(1)} %get-tuple-element.8.other, bf16[1,2304,1536]{2,1,0:T(8,128)(2,1)} %integrals.1), custom_call_target="tpu_custom_call" | custom-call | flops 14495514624 | bytes 41943040 | tf_op jit(solution)/shard_map/ladder/pallas_call | solution.py:275
  166.2 4.3 %swap.1 = bf16[32,64,2304]{2,1,0:T(8,128)(2,1)} custom-call(bf16[64,32,2304]{2,1,0:T(8,128)(2,1)S(1)} %ladder.1.x), custom_call_target="tpu_custom_call" | custom-call | bytes 18874368 | tf_op jit(solution)/shard_map/swap/pallas_call | solution.py:327
Async XLA Ops:
  0.0 4.9 %collective-permute-start = (s32[1]{0:T(128)}, s32[1]{0:T(128)}, u32[]{:S(2)}, u32[]{:S(2)}) collective-permute-start(s32[1]{0:T(128)} %param.8), channel_id=1, source_target_pairs={{0,4},{2,6},{4,0},{6,2},{8,12},{10,14},{12,8},{14,10},{16,20},{18,... | collective-permute-start | bytes 20 | tf_op jit(solution)/shard_map/ppermute | solution.py:344
  4.9 0.7 copy-start

commit v5 on v4

--- a/solution.py
+++ b/solution.py
@@ -22,87 +22,43 @@
 CROSS = N_VV // 2
 MESH = pl.DeviceIdType.MESH
 PART = HALF // 2
-SUB_ROWS = 256
 MIB = 1024 * 1024
 
 
-def slice_kernel(labels, pair, other_pair, panel, amp, own, other, win, buf, in_sem, out_sem):
-    panel_irrep = labels[panel[0] * BS]
-
-    def place(irrep):
-        target = irrep ^ panel_irrep
-        allowed = jnp.int32(0)
-        for k in range(NIRR):
-            allowed += jnp.where(labels[k * BS] == target, jnp.int32(k), jnp.int32(0))
-        tile = jnp.minimum(allowed * BS // 128, 4)
-        return tile, allowed * BS - tile * 128
-
-    mine, theirs = place(pair[0]), place(other_pair[0])
-    parts = [(mine, 0, own, 0), (theirs, HALF // 2, other, 0), (mine, HALF // 2, own, HALF // 2)]
-    units = [(p, q) for p in range(3) for q in range(DW // 4)]
-
-    def window(p, q, j):
-        (tile, _), row, _, _ = parts[p]
-        d = q * 4 + j
-        return pltpu.make_async_copy(
-            amp.at[pl.ds(row, PART), pl.ds(pl.multiple_of(d * NV + tile * 128, 128), 256)],
-            win.at[d, pl.ds(p * PART, PART)],
-            in_sem.at[p, q],
-        )
-
-    def result(p, q):
-        _, _, out, row = parts[p]
-        cols = pl.ds(q * 4 * BS, 4 * BS)
-        return pltpu.make_async_copy(buf.at[pl.ds(p * PART, PART), cols], out.at[pl.ds(row, PART), cols], out_sem.at[p, q])
-
-    for p, q in units:
+def place(labels, panel, irrep):
+    panel_irrep = jnp.int32(0)
+    for k in range(NIRR):
+        panel_irrep += jnp.where(panel == k, labels[k * BS], jnp.int32(0))
+    target = irrep ^ panel_irrep
+    allowed = jnp.int32(0)
+    for k in range(NIRR):
+        allowed += jnp.where(labels[k * BS] == target, jnp.int32(k), jnp.int32(0))
+    return allowed
+
+
+def choose(rows, allowed, out, row):
+    lane = lax.broadcasted_iota(jnp.int32, (CHUNK, 128), 1)
+    upper, rest = allowed // 4, lax.rem(allowed, 4)
+    off = lax.rem(allowed * BS, 128)
+    for q in range(DW // 4):
+        w = []
         for j in range(4):
-            window(p, q, j).start()
-    lane = lax.broadcasted_iota(jnp.int32, (SUB_ROWS, 128), 1)
-
-    for p, q in units:
-        off = parts[p][0][1]
-        for j in range(4):
-            window(p, q, j).wait()
-
-        @pl.loop(0, PART // SUB_ROWS)
-        def _(r):
-            rows = pl.ds(pl.multiple_of(p * PART + r * SUB_ROWS, SUB_ROWS), SUB_ROWS)
-            w = [
-                pltpu.roll(win[q * 4 + j, rows].astype(jnp.float32), lax.rem((96 * j) % 128 - off + 512, 256), 1)
-                for j in range(4)
+            start = (q * 4 + j) * NV
+            t = [
+                jnp.where(upper == 1, rows[:, start + 384 + n : start + 512 + n], rows[:, start + n : start + 128 + n]).astype(jnp.float32)
+                for n in (0, 128, 256)
             ]
-            t0 = jnp.where(lane < 96, w[0][:, :128], w[1][:, :128])
-            t1 = jnp.where(lane < 64, w[1][:, 128:], w[2][:, :128])
-            t2 = jnp.where(lane < 32, w[2][:, 128:], w[3][:, :128])
-            buf[rows, q * 384 : (q + 1) * 384] = jnp.concatenate([t0, t1, t2], axis=1).astype(jnp.bfloat16)
-
-        result(p, q).start()
-    for p, q in units:
-        result(p, q).wait()
-
-
-def slice_blocks(orb, pair, other_pair, panel, amp):
-    smem = pl.BlockSpec(memory_space=pltpu.SMEM)
-    hbm = pl.BlockSpec(memory_space=pl.ANY)
-    return pl.pallas_call(
-        slice_kernel,
-        name="slice_blocks",
-        out_shape=(jax.ShapeDtypeStruct((HALF, KP), jnp.bfloat16), jax.ShapeDtypeStruct((HALF // 2, KP), jnp.bfloat16)),
-        in_specs=[smem, smem, smem, smem, hbm],
-        out_specs=(hbm, hbm),
-        scratch_shapes=[
-            pltpu.VMEM((DW, 3 * PART, 256), jnp.bfloat16),
-            pltpu.VMEM((3 * PART, KP), jnp.bfloat16),
-            pltpu.SemaphoreType.DMA((3, DW // 4)),
-            pltpu.SemaphoreType.DMA((3, DW // 4)),
-        ],
-        compiler_params=pltpu.CompilerParams(vmem_limit_bytes=44 * MIB),
-        cost_estimate=pl.CostEstimate(flops=0, bytes_accessed=3 * PART * 11264, transcendentals=0),
-    )(orb, pair, other_pair, panel, amp)
-
-
-def ladder_kernel(own, other, integrals, recv, a, b, prod, stage, load_sem, give_sem, get_sem, send_sem, recv_sem, self_sem, x_send, x_recv):
+            low = jnp.where(rest < 2, t[0], jnp.where(rest == 2, t[1], t[2]))
+            x = jnp.concatenate([low, jnp.where(rest < 2, t[1], t[2])], axis=1)
+            shift = (96 * j) % 128
+            w.append(pltpu.roll(x, lax.rem(shift - off + 256, 256), 1))
+        t0 = jnp.where(lane < 96, w[0][:, :128], w[1][:, :128])
+        t1 = jnp.where(lane < 64, w[1][:, 128:], w[2][:, :128])
+        t2 = jnp.where(lane < 32, w[2][:, 128:], w[3][:, :128])
+        out[pl.ds(row, CHUNK), q * 384 : (q + 1) * 384] = jnp.concatenate([t0, t1, t2], axis=1).astype(jnp.bfloat16)
+
+
+def ladder_kernel(labels, pair, other_pair, panel, amp, integrals, recv, a, b, prod, stage, other, a0, a1, b0, b1, load_sem, row_sem, give_sem, get_sem, send_sem, recv_sem, self_sem, x_send, x_recv):
     v = lax.axis_index("vv")
     g = lax.axis_index("grp")
     h = 1 - g
@@ -110,10 +66,20 @@
     xh, c = lax.rem(v // 2, 2), lax.rem(v, 2)
     flip = v + 2 - 4 * xh
     turn = 1 - 2 * c
-    load_b = pltpu.make_async_copy(integrals.at[0], b, load_sem.at[0])
-    load_a = pltpu.make_async_copy(own, a.at[pl.ds(g * HALF, HALF)], load_sem.at[1])
-    load_a.start()
-    load_b.start()
+    load_b = pltpu.make_async_copy(integrals.at[0], b, load_sem)
+    held = ((a0, b0), (a1, b1))
+
+    def chunk(j):
+        return pl.multiple_of(lax.rem(y + turn * j + 4, 4) * CHUNK, CHUNK)
+
+    def load(j, parity, part):
+        return pltpu.make_async_copy(
+            amp.at[pl.ds(part * PART + chunk(j), CHUNK)], held[parity][part], row_sem.at[parity, part]
+        )
+
+    for parity in range(2):
+        for part in range(2):
+            load(parity, parity, part).start()
 
     barrier = pltpu.get_barrier_semaphore()
 
@@ -131,31 +97,57 @@
 
     pl.semaphore_wait(barrier, N_VV // 2 + 2)
 
-    n_chunks = HALF // 2 // CHUNK
+    mine = place(labels, panel[0], pair[0])
+    theirs = place(labels, panel[0], other_pair[0])
 
     def gives(j):
+        row = chunk(j)
+        here = a.at[pl.ds(g * HALF + row, CHUNK)]
         first = pltpu.make_async_remote_copy(
-            src_ref=own.at[pl.ds(j * CHUNK, CHUNK)],
-            dst_ref=a.at[pl.ds(g * HALF + j * CHUNK, CHUNK)],
+            src_ref=here,
+            dst_ref=here,
             send_sem=give_sem,
-            recv_sem=get_sem.at[j],
+            recv_sem=get_sem.at[row // CHUNK],
             device_id=(v, h),
             device_id_type=MESH,
         )
         second = pltpu.make_async_remote_copy(
-            src_ref=other.at[pl.ds(j * CHUNK, CHUNK)],
-            dst_ref=a.at[pl.ds(g * HALF + HALF // 2 + j * CHUNK, CHUNK)],
+            src_ref=other.at[pl.ds(row, CHUNK)],
+            dst_ref=a.at[pl.ds(g * HALF + PART + row, CHUNK)],
             send_sem=give_sem,
-            recv_sem=get_sem.at[n_chunks + j],
+            recv_sem=get_sem.at[PART // CHUNK + row // CHUNK],
             device_id=(flip, h),
             device_id_type=MESH,
         )
         return first, second
 
-    for j in range(n_chunks):
-        for copy in gives(lax.rem(y + turn * j + 4, 4)):
-            copy.start()
-    load_a.wait()
+    @pl.loop(0, 2)
+    def _(i):
+        for parity in range(2):
+            j = 2 * i + parity
+            row = chunk(j)
+            first, second = gives(j)
+            load(j, parity, 0).wait()
+            choose(held[parity][0], mine, a, pl.multiple_of(g * HALF + row, CHUNK))
+            first.start()
+
+            @pl.when(i == 0)
+            def _():
+                load(j + 2, parity, 0).start()
+
+            load(j, parity, 1).wait()
+            choose(held[parity][1], theirs, other, row)
+            second.start()
+            choose(held[parity][1], mine, a, pl.multiple_of(g * HALF + PART + row, CHUNK))
+
+            @pl.when(i == 0)
+            def _():
+                load(j + 2, parity, 1).start()
+
+        @pl.when(i == 0)
+        def _():
+            load_b.start()
+
     load_b.wait()
 
     def multiply(row, w0, rows, cols):
@@ -196,7 +188,7 @@
         i = k // 2
         half = lax.rem(z // 2 + k + 1, 2)
         n = lax.rem(i, 4)
-        dy = jnp.where(n == 0, 2, jnp.where(n == 1, 1, jnp.where(n == 2, 3, 0)))
+        dy = lax.rem(n + 1, 4)
         return (2 * half + lax.rem(z + 1 + i // 4, 2)) * 4 + lax.rem(y + turn * dy + 4, 4)
 
     def across(u):
@@ -232,14 +224,10 @@
         multiply(q * CHUNK, q * 4, CHUNK, ROWS)
         near(q)
 
-        @pl.when(i == 6)
-        def _():
-            across(0).start()
-            across(1).start()
-
-    @pl.loop(2, WINDOW)
-    def _(u):
-        across(u).start()
+        @pl.when(i == 4)
+        def _():
+            for u in range(WINDOW):
+                across(u).start()
 
     @pl.loop(0, CROSS)
     def _(u):
@@ -249,7 +237,7 @@
         def _():
             across(u + WINDOW).start()
 
-    for j in range(n_chunks):
+    for j in range(PART // CHUNK):
         for copy in gives(j):
             copy.wait_send()
 
@@ -270,20 +258,27 @@
     rest.wait_recv()
 
 
-def ladder(own, other, integrals):
+def ladder(labels, pair, other_pair, panel, amp, integrals):
     hbm = pl.BlockSpec(memory_space=pl.ANY)
+    smem = pl.BlockSpec(memory_space=pltpu.SMEM)
     return pl.pallas_call(
         ladder_kernel,
         name="ladder",
         out_shape=pltpu.VMEM((N_VV, OWN, ROWS), jnp.bfloat16),
-        in_specs=[hbm] * 3,
+        in_specs=[smem] * 4 + [hbm] * 2,
         out_specs=pl.BlockSpec(memory_space=pltpu.VMEM),
         scratch_shapes=[
             pltpu.VMEM((IJ, KP), jnp.bfloat16),
             pltpu.VMEM((ROWS, KP), jnp.bfloat16),
             pltpu.VMEM((N_VV, OWN, ROWS), jnp.bfloat16),
             pltpu.VMEM((N_VV // 2, OWN, ROWS), jnp.bfloat16),
-            pltpu.SemaphoreType.DMA((2,)),
+            pltpu.VMEM((PART, KP), jnp.bfloat16),
+            pltpu.VMEM((CHUNK, DW * NV), jnp.bfloat16),
+            pltpu.VMEM((CHUNK, DW * NV), jnp.bfloat16),
+            pltpu.VMEM((CHUNK, DW * NV), jnp.bfloat16),
+            pltpu.VMEM((CHUNK, DW * NV), jnp.bfloat16),
+            pltpu.SemaphoreType.DMA,
+            pltpu.SemaphoreType.DMA((2, 2)),
             pltpu.SemaphoreType.DMA,
             pltpu.SemaphoreType.DMA((HALF // CHUNK,)),
             pltpu.SemaphoreType.DMA,
@@ -293,10 +288,10 @@
             pltpu.SemaphoreType.DMA((CROSS,)),
         ],
         compiler_params=pltpu.CompilerParams(
-            collective_id=0, has_side_effects=True, vmem_limit_bytes=40 * MIB
+            collective_id=0, has_side_effects=True, vmem_limit_bytes=48 * MIB
         ),
-        cost_estimate=pl.CostEstimate(flops=2 * IJ * ROWS * KP, bytes_accessed=40 * MIB, transcendentals=0),
-    )(own, other, integrals)
+        cost_estimate=pl.CostEstimate(flops=2 * IJ * ROWS * KP, bytes_accessed=60 * MIB, transcendentals=0),
+    )(labels, pair, other_pair, panel, amp, integrals)
 
 
 TCOL = 768
@@ -342,8 +337,7 @@
 def shards(integrals, amplitudes, orbital_irrep, pair_irrep, panel_block):
     flipped = [(i, i ^ 2) for i in range(N_VV)]
     other_irrep = lax.ppermute(pair_irrep, "vv", flipped)
-    own, other = slice_blocks(orbital_irrep, pair_irrep, other_irrep, panel_block, amplitudes)
-    return swap(ladder(own, other, integrals))
+    return swap(ladder(orbital_irrep, pair_irrep, other_irrep, panel_block, amplitudes, integrals))
 
 
 def solution(mesh):

time: 172 us -> 171 us (level)
    pallas_call x1 -> x0, Pallas kernels: 9.14 us -> none  [slice_blocks(): pl.pallas_call(slice_kernel, name='slice_blocks', out_shape=(jax.ShapeDty...]
    pallas_call x1, Pallas kernels: 151 us -> 160 us  [ladder(): pl.pallas_call(ladder_kernel, name='ladder', out_shape=pltpu.VMEM((N_VV,...]
where the time goes in v5:
time: 171 us; the launch traced here: 169 us
  Pallas kernels  164 us (96%)
  starting transfers between devices  3.57 us (2%)
    pallas_call x1, Pallas kernels, ladder(): pl.pallas_call(ladder_kernel, name='ladder', out_shape=pltpu.VMEM((N_VV,...  160 us
    pallas_call x1, Pallas kernels, swap(): pl.pallas_call(swap_kernel, name='swap', out_shape=jax.ShapeDtypeStruct((...  4.27 us
    ppermute x1, starting transfers between devices, shards(): other_irrep = lax.ppermute(pair_irrep, 'vv', flipped)  3.57 us
  transfers between devices with their start and end apart: 1, of which 0 were waited for; matrix products, arithmetic and copies ran while one was open for 0% of the time, Pallas kernels for 0%

profile of v5, /device:TPU:1, one launch (start us, length us, event | category | flops | bytes accessed | tf_op | source)
XLA Modules:
  0.0 169.0 jit_solution(8459823368499593886)
XLA Ops:
  0.0 3.6 %collective-permute-start = (s32[1]{0:T(128)}, s32[1]{0:T(128)}, u32[]{:S(2)}, u32[]{:S(2)}) collective-permute-start(s32[1]{0:T(128)} %param.8), channel_id=1, source_target_pairs={{0,4},{2,6},{4,0},{6,2},{8,12},{10,14},{12,8},{14,10},{16,20},{18,... | collective-permute-start | bytes 20 | tf_op jit(solution)/shard_map/ppermute | solution.py:339
  4.9 0.0 collective-permute-done.other_pair
  4.9 159.8 %ladder.1.x = bf16[64,32,2304]{2,1,0:T(8,128)(2,1)S(1)} custom-call(s32[768]{0:T(1024)} %labels.1, s32[1]{0:T(128)S(6)} %copy.6.pair, s32[1]{0:T(128)} %collective-permute-done.other_pair, s32[1]{0:T(128)S(6)} %copy.7.panel, bf16[1024,12288]{1,0:T(8,128)(2,1)} %amp.1, bf16[1,2304,1536]{2,1,0:T(8,128)(2,1)} %integrals.1), custom_call_target="tpu_custom_call" | custom-call | flops 14495514624 | bytes 62914560 | tf_op jit(solution)/shard_map/ladder/pallas_call | solution.py:264
  164.8 4.3 %swap.1 = bf16[32,64,2304]{2,1,0:T(8,128)(2,1)} custom-call(bf16[64,32,2304]{2,1,0:T(8,128)(2,1)S(1)} %ladder.1.x), custom_call_target="tpu_custom_call" | custom-call | bytes 18874368 | tf_op jit(solution)/shard_map/swap/pallas_call | solution.py:322
Async XLA Ops:
  0.0 4.9 %collective-permute-start = (s32[1]{0:T(128)}, s32[1]{0:T(128)}, u32[]{:S(2)}, u32[]{:S(2)}) collective-permute-start(s32[1]{0:T(128)} %param.8), channel_id=1, source_target_pairs={{0,4},{2,6},{4,0},{6,2},{8,12},{10,14},{12,8},{14,10},{16,20},{18,... | collective-permute-start | bytes 20 | tf_op jit(solution)/shard_map/ppermute | solution.py:339

commit v6 on v5

--- a/solution.py
+++ b/solution.py
@@ -20,6 +20,7 @@
 CHUNK = 128
 WINDOW = 4
 CROSS = N_VV // 2
+COLS = 768
 MESH = pl.DeviceIdType.MESH
 PART = HALF // 2
 MIB = 1024 * 1024
@@ -77,9 +78,11 @@
             amp.at[pl.ds(part * PART + chunk(j), CHUNK)], held[parity][part], row_sem.at[parity, part]
         )
 
-    for parity in range(2):
-        for part in range(2):
-            load(parity, parity, part).start()
+    load(0, 0, 0).start()
+    load(0, 0, 1).start()
+    load_b.start()
+    load(1, 1, 0).start()
+    load(1, 1, 1).start()
 
     barrier = pltpu.get_barrier_semaphore()
 
@@ -121,46 +124,17 @@
         )
         return first, second
 
-    @pl.loop(0, 2)
-    def _(i):
-        for parity in range(2):
-            j = 2 * i + parity
-            row = chunk(j)
-            first, second = gives(j)
-            load(j, parity, 0).wait()
-            choose(held[parity][0], mine, a, pl.multiple_of(g * HALF + row, CHUNK))
-            first.start()
-
-            @pl.when(i == 0)
-            def _():
-                load(j + 2, parity, 0).start()
-
-            load(j, parity, 1).wait()
-            choose(held[parity][1], theirs, other, row)
-            second.start()
-            choose(held[parity][1], mine, a, pl.multiple_of(g * HALF + PART + row, CHUNK))
-
-            @pl.when(i == 0)
-            def _():
-                load(j + 2, parity, 1).start()
-
-        @pl.when(i == 0)
-        def _():
-            load_b.start()
-
-    load_b.wait()
-
-    def multiply(row, w0, rows, cols):
-        @pl.loop(0, ROWS // cols)
+    def multiply(q0, q1):
+        @pl.loop(0, ROWS // COLS)
         def _(n):
-            col = pl.multiple_of(n * cols, cols)
+            col = pl.multiple_of(n * COLS, COLS)
+            rows = jnp.concatenate([a[pl.ds(pl.multiple_of(q * CHUNK, CHUNK), CHUNK), :] for q in (q0, q1)], axis=0)
             part = lax.dot_general(
-                a[pl.ds(pl.multiple_of(row, rows), rows), :],
-                b[pl.ds(col, cols), :],
-                (((1,), (1,)), ((), ())),
-                preferred_element_type=jnp.float32,
+                rows, b[pl.ds(col, COLS), :], (((1,), (1,)), ((), ())), preferred_element_type=jnp.float32
             )
-            prod[pl.ds(w0, rows // OWN), :, pl.ds(col, cols)] = part.astype(jnp.bfloat16).reshape(rows // OWN, OWN, cols)
+            part = part.astype(jnp.bfloat16).reshape(8, OWN, COLS)
+            prod[pl.ds(q0 * 4, 4), :, pl.ds(col, COLS)] = part[:4]
+            prod[pl.ds(q1 * 4, 4), :, pl.ds(col, COLS)] = part[4:]
 
     def push(source, w, sender):
         @pl.when(w == v)
@@ -209,22 +183,52 @@
 
     @pl.loop(0, 2)
     def _(i):
-        zz = 2 * g + lax.rem(z + i, 2)
-        multiply(zz * 512, zz * 16, 512, 768)
-
-        @pl.loop(0, 4)
-        def _(j):
-            near(zz * 4 + lax.rem(y + turn * j + 4, 4))
-
-    @pl.loop(0, HALF // CHUNK)
+        for parity in range(2):
+            j = 2 * i + parity
+            row = chunk(j)
+            first, second = gives(j)
+            load(j, parity, 0).wait()
+            choose(held[parity][0], mine, a, pl.multiple_of(g * HALF + row, CHUNK))
+            first.start()
+
+            @pl.when(i == 0)
+            def _():
+                load(j + 2, parity, 0).start()
+
+            load(j, parity, 1).wait()
+            choose(held[parity][1], theirs, other, row)
+            second.start()
+            choose(held[parity][1], mine, a, pl.multiple_of(g * HALF + PART + row, CHUNK))
+
+            @pl.when(i == 0)
+            def _():
+                load(j + 2, parity, 1).start()
+
+            if parity == 0:
+
+                @pl.when(i == 0)
+                def _():
+                    load_b.wait()
+
+            mine_at = 8 * g + row // CHUNK
+            multiply(mine_at, mine_at + 4)
+            near(mine_at + 4 * lax.rem(z, 2))
+            near(mine_at + 4 * lax.rem(z + 1, 2))
+
+    @pl.loop(0, 4)
     def _(i):
-        q = (2 * h + lax.rem(i + z, 2)) * 4 + lax.rem(y + turn * (i // 2) + 4, 4)
-        here = a.at[pl.ds(q * CHUNK, CHUNK)]
-        pltpu.make_async_remote_copy(here, here, give_sem, get_sem.at[q - 8 * h], device_id=(v, h), device_id_type=MESH).wait_recv()
-        multiply(q * CHUNK, q * 4, CHUNK, ROWS)
-        near(q)
-
-        @pl.when(i == 4)
+        y4 = lax.rem(y + turn * i + 4, 4)
+        for s in range(2):
+            q = 8 * h + 4 * s + y4
+            here = a.at[pl.ds(q * CHUNK, CHUNK)]
+            pltpu.make_async_remote_copy(
+                here, here, give_sem, get_sem.at[4 * s + y4], device_id=(v, h), device_id_type=MESH
+            ).wait_recv()
+        multiply(8 * h + y4, 8 * h + 4 + y4)
+        near(8 * h + 4 * lax.rem(z, 2) + y4)
+        near(8 * h + 4 * lax.rem(z + 1, 2) + y4)
+
+        @pl.when(i == 3)
         def _():
             for u in range(WINDOW):
                 across(u).start()

time: 171 us -> 163 us (0.953); the launches traced: 169 us -> 163 us
  Pallas kernels: 164 us -> 158 us
    pallas_call x1, Pallas kernels: 160 us -> 154 us  [ladder(): pl.pallas_call(ladder_kernel, name='ladder', out_shape=pltpu.VMEM((N_VV,...]
where the time goes in v6:
time: 163 us
  Pallas kernels  158 us (97%)
  starting transfers between devices  3.57 us (2%)
    pallas_call x1, Pallas kernels, ladder(): pl.pallas_call(ladder_kernel, name='ladder', out_shape=pltpu.VMEM((N_VV,...  154 us
    pallas_call x1, Pallas kernels, swap(): pl.pallas_call(swap_kernel, name='swap', out_shape=jax.ShapeDtypeStruct((...  4.27 us
    ppermute x1, starting transfers between devices, shards(): other_irrep = lax.ppermute(pair_irrep, 'vv', flipped)  3.57 us
  transfers between devices with their start and end apart: 1, of which 0 were waited for; matrix products, arithmetic and copies ran while one was open for 0% of the time, Pallas kernels for 0%

profile of v6, /device:TPU:1, one launch (start us, length us, event | category | flops | bytes accessed | tf_op | source)
XLA Modules:
  0.0 162.8 jit_solution(13254090571888576679)
XLA Ops:
  0.0 3.6 %collective-permute-start = (s32[1]{0:T(128)}, s32[1]{0:T(128)}, u32[]{:S(2)}, u32[]{:S(2)}) collective-permute-start(s32[1]{0:T(128)} %param.8), channel_id=1, source_target_pairs={{0,4},{2,6},{4,0},{6,2},{8,12},{10,14},{12,8},{14,10},{16,20},{18,... | collective-permute-start | bytes 20 | tf_op jit(solution)/shard_map/ppermute | solution.py:343
  4.9 0.0 collective-permute-done.other_pair
  4.9 153.6 %ladder.1.x = bf16[64,32,2304]{2,1,0:T(8,128)(2,1)S(1)} custom-call(s32[768]{0:T(1024)} %labels.1, s32[1]{0:T(128)S(6)} %copy.6.pair, s32[1]{0:T(128)} %collective-permute-done.other_pair, s32[1]{0:T(128)S(6)} %copy.7.panel, bf16[1024,12288]{1,0:T(8,128)(2,1)} %amp.1, bf16[1,2304,1536]{2,1,0:T(8,128)(2,1)} %integrals.1), custom_call_target="tpu_custom_call" | custom-call | flops 14495514624 | bytes 62914560 | tf_op jit(solution)/shard_map/ladder/pallas_call | solution.py:268
  158.5 4.3 %swap.1 = bf16[32,64,2304]{2,1,0:T(8,128)(2,1)} custom-call(bf16[64,32,2304]{2,1,0:T(8,128)(2,1)S(1)} %ladder.1.x), custom_call_target="tpu_custom_call" | custom-call | bytes 18874368 | tf_op jit(solution)/shard_map/swap/pallas_call | solution.py:326
Async XLA Ops:
  0.0 4.9 %collective-permute-start = (s32[1]{0:T(128)}, s32[1]{0:T(128)}, u32[]{:S(2)}, u32[]{:S(2)}) collective-permute-start(s32[1]{0:T(128)} %param.8), channel_id=1, source_target_pairs={{0,4},{2,6},{4,0},{6,2},{8,12},{10,14},{12,8},{14,10},{16,20},{18,... | collective-permute-start | bytes 20 | tf_op jit(solution)/shard_map/ppermute | solution.py:343

commit v7 on v6

--- a/solution.py
+++ b/solution.py
@@ -59,7 +59,7 @@
         out[pl.ds(row, CHUNK), q * 384 : (q + 1) * 384] = jnp.concatenate([t0, t1, t2], axis=1).astype(jnp.bfloat16)
 
 
-def ladder_kernel(labels, pair, other_pair, panel, amp, integrals, recv, a, b, prod, stage, other, a0, a1, b0, b1, load_sem, row_sem, give_sem, get_sem, send_sem, recv_sem, self_sem, x_send, x_recv):
+def ladder_kernel(labels, pair, panel, amp, integrals, recv, a, b, prod, stage, other, a0, a1, b0, b1, tag_out, tag_in, tag_sem, load_sem, row_sem, give_sem, get_sem, send_sem, recv_sem, self_sem, x_send, x_recv):
     v = lax.axis_index("vv")
     g = lax.axis_index("grp")
     h = 1 - g
@@ -84,6 +84,7 @@
     load(1, 1, 0).start()
     load(1, 1, 1).start()
 
+    tag_out[...] = jnp.full((8, 128), pair[0], jnp.int32)
     barrier = pltpu.get_barrier_semaphore()
 
     def greet(w, group):
@@ -100,8 +101,16 @@
 
     pl.semaphore_wait(barrier, N_VV // 2 + 2)
 
+    tag = pltpu.make_async_remote_copy(
+        src_ref=tag_out,
+        dst_ref=tag_in,
+        send_sem=tag_sem.at[0],
+        recv_sem=tag_sem.at[1],
+        device_id=(flip, g),
+        device_id_type=MESH,
+    )
+    tag.start()
     mine = place(labels, panel[0], pair[0])
-    theirs = place(labels, panel[0], other_pair[0])
 
     def gives(j):
         row = chunk(j)
@@ -163,7 +172,7 @@
         half = lax.rem(z // 2 + k + 1, 2)
         n = lax.rem(i, 4)
         dy = lax.rem(n + 1, 4)
-        return (2 * half + lax.rem(z + 1 + i // 4, 2)) * 4 + lax.rem(y + turn * dy + 4, 4)
+        return (2 * half + lax.rem(z + k + i // 4, 2)) * 4 + lax.rem(y + turn * dy + 4, 4)
 
     def across(u):
         q, core = crossing(u // 2), lax.rem(c + u + 1, 2)
@@ -177,27 +186,39 @@
         )
 
     def forward(u):
-        across(u).wait_recv()
         q, core = crossing(u // 2), lax.rem(c + u + 1, 2)
         push(stage.at[q * 2 + core], q * 4 + xh * 2 + core, flip)
+
+    def first_part(j, parity):
+        load(j, parity, 0).wait()
+        choose(held[parity][0], mine, a, pl.multiple_of(g * HALF + chunk(j), CHUNK))
+        gives(j)[0].start()
+
+    first_part(0, 0)
+    load(2, 0, 0).start()
+    tag.wait()
+    theirs = place(labels, panel[0], jnp.max(tag_in[...]))
 
     @pl.loop(0, 2)
     def _(i):
         for parity in range(2):
             j = 2 * i + parity
             row = chunk(j)
-            first, second = gives(j)
-            load(j, parity, 0).wait()
-            choose(held[parity][0], mine, a, pl.multiple_of(g * HALF + row, CHUNK))
-            first.start()
-
-            @pl.when(i == 0)
-            def _():
-                load(j + 2, parity, 0).start()
+            if parity == 0:
+
+                @pl.when(i == 1)
+                def _():
+                    first_part(2, 0)
+            else:
+                first_part(j, 1)
+
+                @pl.when(i == 0)
+                def _():
+                    load(3, 1, 0).start()
 
             load(j, parity, 1).wait()
             choose(held[parity][1], theirs, other, row)
-            second.start()
+            gives(j)[1].start()
             choose(held[parity][1], mine, a, pl.multiple_of(g * HALF + PART + row, CHUNK))
 
             @pl.when(i == 0)
@@ -235,11 +256,13 @@
 
     @pl.loop(0, CROSS)
     def _(u):
-        forward(u)
+        across(u).wait_recv()
 
         @pl.when(u + WINDOW < CROSS)
         def _():
             across(u + WINDOW).start()
+
+        forward(u)
 
     for j in range(PART // CHUNK):
         for copy in gives(j):
@@ -262,14 +285,14 @@
     rest.wait_recv()
 
 
-def ladder(labels, pair, other_pair, panel, amp, integrals):
+def ladder(labels, pair, panel, amp, integrals):
     hbm = pl.BlockSpec(memory_space=pl.ANY)
     smem = pl.BlockSpec(memory_space=pltpu.SMEM)
     return pl.pallas_call(
         ladder_kernel,
         name="ladder",
         out_shape=pltpu.VMEM((N_VV, OWN, ROWS), jnp.bfloat16),
-        in_specs=[smem] * 4 + [hbm] * 2,
+        in_specs=[smem] * 3 + [hbm] * 2,
         out_specs=pl.BlockSpec(memory_space=pltpu.VMEM),
         scratch_shapes=[
             pltpu.VMEM((IJ, KP), jnp.bfloat16),
@@ -281,6 +304,9 @@
             pltpu.VMEM((CHUNK, DW * NV), jnp.bfloat16),
             pltpu.VMEM((CHUNK, DW * NV), jnp.bfloat16),
             pltpu.VMEM((CHUNK, DW * NV), jnp.bfloat16),
+            pltpu.VMEM((8, 128), jnp.int32),
+            pltpu.VMEM((8, 128), jnp.int32),
+            pltpu.SemaphoreType.DMA((2,)),
             pltpu.SemaphoreType.DMA,
             pltpu.SemaphoreType.DMA((2, 2)),
             pltpu.SemaphoreType.DMA,
@@ -295,7 +321,7 @@
             collective_id=0, has_side_effects=True, vmem_limit_bytes=48 * MIB
         ),
         cost_estimate=pl.CostEstimate(flops=2 * IJ * ROWS * KP, bytes_accessed=60 * MIB, transcendentals=0),
-    )(labels, pair, other_pair, panel, amp, integrals)
+    )(labels, pair, panel, amp, integrals)
 
 
 TCOL = 768
@@ -339,9 +365,7 @@
 
 
 def shards(integrals, amplitudes, orbital_irrep, pair_irrep, panel_block):
-    flipped = [(i, i ^ 2) for i in range(N_VV)]
-    other_irrep = lax.ppermute(pair_irrep, "vv", flipped)
-    return swap(ladder(orbital_irrep, pair_irrep, other_irrep, panel_block, amplitudes, integrals))
+    return swap(ladder(orbital_irrep, pair_irrep, panel_block, amplitudes, integrals))
 
 
 def solution(mesh):

time: 163 us -> 160 us (0.982)
  starting transfers between devices: 3.57 us -> 0 us
    ppermute x1 -> x0, starting transfers between devices: 3.57 us -> none  [shards(): other_irrep = lax.ppermute(pair_irrep, 'vv', flipped)]
  transfers between devices with their start and end apart: 1 -> 0, of which waited for: 0 -> 0; matrix products, arithmetic and copies ran while one was open for 0% -> 0% of each run, Pallas kernels for 0% -> 0%
where the time goes in v7:
time: 160 us
  Pallas kernels  159 us (99%)
    pallas_call x1, Pallas kernels, ladder(): pl.pallas_call(ladder_kernel, name='ladder', out_shape=pltpu.VMEM((N_VV,...  154 us
    pallas_call x1, Pallas kernels, swap(): pl.pallas_call(swap_kernel, name='swap', out_shape=jax.ShapeDtypeStruct((...  4.27 us

profile of v7, /device:TPU:1, one launch (start us, length us, event | category | flops | bytes accessed | tf_op | source)
XLA Modules:
  0.0 159.9 jit_solution(810707804752897645)
XLA Ops:
  1.3 154.4 %ladder.1.x = bf16[64,32,2304]{2,1,0:T(8,128)(2,1)S(1)} custom-call(s32[768]{0:T(1024)} %labels.1, s32[1]{0:T(128)S(6)} %copy.6.pair, s32[1]{0:T(128)S(6)} %copy.7.panel, bf16[1024,12288]{1,0:T(8,128)(2,1)} %amp.1, bf16[1,2304,1536]{2,1,0:T(8,128)(2,1)} %integrals.1), custom_call_target="tpu_custom_call" | custom-call | flops 14495514624 | bytes 62914560 | tf_op jit(solution)/shard_map/ladder/pallas_call | solution.py:291
  155.7 4.3 %swap.1 = bf16[32,64,2304]{2,1,0:T(8,128)(2,1)} custom-call(bf16[64,32,2304]{2,1,0:T(8,128)(2,1)S(1)} %ladder.1.x), custom_call_target="tpu_custom_call" | custom-call | bytes 18874368 | tf_op jit(solution)/shard_map/swap/pallas_call | solution.py:352

commit v8 on v7

--- a/solution.py
+++ b/solution.py
@@ -59,7 +59,7 @@
         out[pl.ds(row, CHUNK), q * 384 : (q + 1) * 384] = jnp.concatenate([t0, t1, t2], axis=1).astype(jnp.bfloat16)
 
 
-def ladder_kernel(labels, pair, panel, amp, integrals, recv, a, b, prod, stage, other, a0, a1, b0, b1, tag_out, tag_in, tag_sem, load_sem, row_sem, give_sem, get_sem, send_sem, recv_sem, self_sem, x_send, x_recv):
+def ladder_kernel(labels, pair, panel, amp, integrals, recv, a, b, prod, stage, other, a0, a1, b0, b1, tag_out, tag_in, tag_sem, ready_sem, load_sem, row_sem, give_sem, get_sem, send_sem, recv_sem, self_sem, x_send, x_recv):
     v = lax.axis_index("vv")
     g = lax.axis_index("grp")
     h = 1 - g
@@ -245,14 +245,21 @@
             pltpu.make_async_remote_copy(
                 here, here, give_sem, get_sem.at[4 * s + y4], device_id=(v, h), device_id_type=MESH
             ).wait_recv()
+
+        @pl.when(i == 3)
+        def _():
+            for w, group in ((v, h), (flip, h), (flip, g)):
+                pl.semaphore_signal(ready_sem, inc=1, device_id=(w, group), device_id_type=MESH)
+
+        @pl.when(i == 3)
+        def _():
+            pl.semaphore_wait(ready_sem, 3)
+            for u in range(WINDOW):
+                across(u).start()
+
         multiply(8 * h + y4, 8 * h + 4 + y4)
         near(8 * h + 4 * lax.rem(z, 2) + y4)
         near(8 * h + 4 * lax.rem(z + 1, 2) + y4)
-
-        @pl.when(i == 3)
-        def _():
-            for u in range(WINDOW):
-                across(u).start()
 
     @pl.loop(0, CROSS)
     def _(u):
@@ -307,6 +314,7 @@
             pltpu.VMEM((8, 128), jnp.int32),
             pltpu.VMEM((8, 128), jnp.int32),
             pltpu.SemaphoreType.DMA((2,)),
+            pltpu.SemaphoreType.REGULAR,
             pltpu.SemaphoreType.DMA,
             pltpu.SemaphoreType.DMA((2, 2)),
             pltpu.SemaphoreType.DMA,

time: 160 us -> 159 us (level)
  no operation moved by 1% of the time
where the time goes in v8:
time: 159 us
  Pallas kernels  158 us (99%)
    pallas_call x1, Pallas kernels, ladder(): pl.pallas_call(ladder_kernel, name='ladder', out_shape=pltpu.VMEM((N_VV,...  154 us
    pallas_call x1, Pallas kernels, swap(): pl.pallas_call(swap_kernel, name='swap', out_shape=jax.ShapeDtypeStruct((...  4.27 us

profile of v8, /device:TPU:1, one launch (start us, length us, event | category | flops | bytes accessed | tf_op | source)
XLA Modules:
  0.0 159.2 jit_solution(1460531974963501245)
XLA Ops:
  1.3 153.6 %ladder.1.x = bf16[64,32,2304]{2,1,0:T(8,128)(2,1)S(1)} custom-call(s32[768]{0:T(1024)} %labels.1, s32[1]{0:T(128)S(6)} %copy.6.pair, s32[1]{0:T(128)S(6)} %copy.7.panel, bf16[1024,12288]{1,0:T(8,128)(2,1)} %amp.1, bf16[1,2304,1536]{2,1,0:T(8,128)(2,1)} %integrals.1), custom_call_target="tpu_custom_call" | custom-call | flops 14495514624 | bytes 62914560 | tf_op jit(solution)/shard_map/ladder/pallas_call | solution.py:298
  154.9 4.3 %swap.1 = bf16[32,64,2304]{2,1,0:T(8,128)(2,1)} custom-call(bf16[64,32,2304]{2,1,0:T(8,128)(2,1)S(1)} %ladder.1.x), custom_call_target="tpu_custom_call" | custom-call | bytes 18874368 | tf_op jit(solution)/shard_map/swap/pallas_call | solution.py:360
